TPU v7x, 256 devices: a whole 4x4x8 slice. The times are simulated.
256 devices in a mesh: wide: 32 (over x, z), narrow: 8 (over y, core).
Axes of the slice: x: 4, y: 4, z: 8, core: 2. Of those that a mesh axis runs over, the one named last changes fastest.
Arguments:
- residual: bfloat16 [256, 768, 1024], P(('wide', 'narrow')), may hold values from -6 to 6
- share: bfloat16 [256, 1024], P(('wide', 'narrow')), may hold values from 0.19921875 to 0.796875
- orient: int32 [256, 2, 512], P(('wide', 'narrow')), may hold values from 0 to 511, each once within a row
- local_inverse: bfloat16 [256, 2048, 2048], P(('wide', 'narrow')), may hold values from -2 to 5, as said below
- primal_basis: bfloat16 [256, 24, 2048], P(('wide', 'narrow')), may hold values from -0.29882812 to 0.29882812
- primal_index: int32 [256, 24], replicated, may hold values from 0 to 2303
- coarse_inverse: float32 [2304, 2304], P(('wide', 'narrow')), may hold values from -1 to 4, as said below
Outputs:
- assembled: bfloat16 [256, 768, 1024], P(('wide', 'narrow'))
Inputs may be any that keep to these rules, and one draw needn't show every extreme that they name: `orient`: each row is a permutation of 0 to 511. `local_inverse`: each patch's matrix is symmetric positive definite. `coarse_inverse`: symmetric positive definite.
All inputs are finite; a program needn't handle non-finite values.
Results may differ from a plain program's by a relative error of at most 0.0056.
Values may be sent and summed in bfloat16 or wider, within the bound.
No kernel may reach another device: no remote copies, remote signals or barrier semaphores. Data moves between devices by JAX's collectives and lax.ppermute only.
A program may use at most 128 MiB of HBM per device.

v0:
```python
import jax
import jax.numpy as jnp
from jax import lax
from jax.sharding import PartitionSpec as P


def as_sent(array):
    return jax.tree.map(lambda a: a.astype(jnp.bfloat16) if a.dtype == jnp.float32 else a, array)


def from_behind(array, axis, by):
    devices = lax.axis_size(axis)
    return lax.ppermute(array, axis, [(i, (i + by) % devices) for i in range(devices)])


def over_wide(payload, steps):
    return jax.tree.map(
        lambda part, own: part.astype(own.dtype),
        from_behind(as_sent(payload), "wide", steps),
        payload,
    )


def over_narrow(payload, steps):
    return jax.tree.map(
        lambda part, own: part.astype(own.dtype),
        from_behind(as_sent(payload), "narrow", steps),
        payload,
    )


def inverse_order(order):
    count = order.shape[0]
    return jnp.zeros((count,), jnp.int32).at[order].set(jnp.arange(count, dtype=jnp.int32))


def on_device(residual, share, orient, local_inverse, primal_basis, primal_index, coarse_inverse):
    res = residual[0]
    shr = share[0]
    ori = orient[0]
    inverse = local_inverse[0]
    basis = primal_basis[0]
    face = res.shape[1] // 2
    got_wide, shr_wide = over_wide((res[:, :face], shr[:face]), 1)
    got_nar, shr_nar = over_narrow((res[:, face:], shr[face:]), 1)
    got_wide = jnp.take(got_wide, ori[0], axis=1)
    got_nar = jnp.take(got_nar, ori[1], axis=1)
    wt_wide = jnp.take(shr_wide, ori[0]).astype(jnp.float32)
    wt_nar = jnp.take(shr_nar, ori[1]).astype(jnp.float32)
    weights = jnp.concatenate([shr.astype(jnp.float32), 1.0 - wt_wide, 1.0 - wt_nar])
    values = jnp.concatenate([res, got_wide, got_nar], axis=1)
    gathered = (weights[None, :] * values.astype(jnp.float32)).astype(jnp.bfloat16)
    primal = jnp.dot(gathered, basis.T, preferred_element_type=jnp.float32)
    patch_id = lax.axis_index("wide") * lax.axis_size("narrow") + lax.axis_index("narrow")
    my_index = lax.dynamic_slice_in_dim(primal_index, patch_id, 1, 0)[0]
    coarse_cols = coarse_inverse.shape[1]
    columns = jnp.arange(coarse_cols, dtype=jnp.int32)
    selector = (my_index[:, None] == columns[None, :]).astype(jnp.float32)
    partial_rhs = jnp.dot(primal, selector, precision=lax.Precision.HIGHEST)
    coarse_rhs = lax.psum(partial_rhs, ("wide", "narrow"))
    own_rows = jnp.dot(coarse_rhs, coarse_inverse.T, precision=lax.Precision.HIGHEST)
    coarse_corr = lax.all_gather(own_rows, ("wide", "narrow"), axis=1, tiled=True)
    patch_corr = jnp.dot(coarse_corr, selector.T, precision=lax.Precision.HIGHEST)
    local = jnp.dot(gathered, inverse, preferred_element_type=jnp.float32)
    coarse_part = jnp.dot(patch_corr, basis.astype(jnp.float32), precision=lax.Precision.HIGHEST)
    weighted = (weights[None, :] * (local + coarse_part)).astype(jnp.bfloat16)
    sent_wide = jnp.take(weighted[:, 2 * face : 3 * face], inverse_order(ori[0]), axis=1)
    sent_nar = jnp.take(weighted[:, 3 * face :], inverse_order(ori[1]), axis=1)
    back_wide = over_wide(sent_wide, -1).astype(jnp.float32)
    back_nar = over_narrow(sent_nar, -1).astype(jnp.float32)
    own = weighted[:, : 2 * face].astype(jnp.float32)
    total = own + jnp.concatenate([back_wide, back_nar], axis=1)
    return total.astype(jnp.bfloat16)[None]


def solution(mesh):
    placed = (
        P(("wide", "narrow"), None, None),
        P(("wide", "narrow"), None),
        P(("wide", "narrow"), None, None),
        P(("wide", "narrow"), None, None),
        P(("wide", "narrow"), None, None),
        P(),
        P(("wide", "narrow"), None),
    )
    return jax.shard_map(
        on_device,
        mesh=mesh,
        in_specs=placed,
        out_specs=P(("wide", "narrow"), None, None),
        check_vma=False,
    )
```

profile of v0, /device:TPU:1, one launch (start us, length us, event | category | flops | bytes accessed | tf_op | source)
XLA Modules:
  0.0 506.5 jit_solution(5462851849851792136)
XLA Ops:
  7.3 2.5 collective-permute-start
  9.8 2.1 collective-permute-start.1
  12.0 2.4 fusion.17
  18.6 3.5 gather_fusion
  22.2 3.5 gather_fusion.1
  25.7 11.3 %collective-permute-done.2 = bf16[768,512]{1,0:T(8,128)(2,1)S(1)} collective-permute-done((bf16[768,512]{1,0:T(8,128)(2,1)S(1)}, bf16[768,512]{1,0:T(8,128)(2,1)S(1)}, u32[]{:S(2)}, u32[]{:S(2)}) %collective-permute-start.2) | collective-permute-done | bytes 786464 | tf_op jit(solution)/shard_map/ppermute | solution.py:13
  37.3 2.0 gather_fusion.2
  39.9 2.0 gather_fusion.3
  42.4 2.3 fusion.3
  44.7 5.1 %fusion.5 = f32[768,2304]{1,0:T(8,128)} fusion(f32[768,24]{0,1:T(8,128)S(1)} %fusion.3, s32[24]{0:T(128)S(1)} %dynamic-slice_reduce_fusion), kind=kOutput, calls=%fused_computation.22 | convolution fusion | flops 509663232 | bytes 7151712 | tf_op jit(solution)/shard_map/dot_general | solution.py:59
  49.9 273.1 %all-reduce.2.cloned.1.call-done = f32[768,2304]{1,0:T(8,128)} async-done(((f32[768,2304]{1,0:T(8,128)}), f32[768,2304]{1,0:T(8,128)}) %all-reduce.2.cloned.1.call-update) | async-done | bytes 7077904 | tf_op jit(solution)/shard_map/psum | solution.py:60
  323.0 8.6 %convolution_bitcast_fusion = f32[1,9,768]{2,1,0:T(8,128)} fusion(f32[768,2304]{1,0:T(8,128)} %all-reduce.2.cloned.1.call-done, f32[9,2304]{1,0:T(8,128)S(1)} %copy-done), kind=kOutput, calls=%fused_computation.14 | convolution fusion | flops 191102976 | bytes 7188480 | tf_op jit(solution)/shard_map/dot_general | solution.py:61
  331.6 2.6 scatter_custom_fusion
  334.3 2.4 scatter_custom_fusion.1
  336.8 10.7 %fusion = f32[768,2048]{1,0:T(8,128)} fusion(bf16[1,2048,2048]{2,1,0:T(8,128)(2,1)} %param.14, bf16[768,512]{1,0:T(8,128)(2,1)S(1)} %get-tuple-element.21, bf16[768,512]{1,0:T(8,128)(2,1)S(1)} %get-tuple-element.22, bf16[768,1024]{1,0:T(8,128)(2,1)S(1)} %bitcast.39, f32[2048]{0:T(1024)S(1)} %pad_maximum_fusion), kind=kOutput, calls=%fused_computation.8 | convolution fusion | flops 6455033856 | bytes 17833984 | tf_op jit(solution)/shard_map/dot_general | solution.py:64
  347.5 105.5 %all-gather.3.cloned.1.call-done = f32[256,9,768]{2,1,0:T(8,128)} async-done(((f32[1,9,768]{2,1,0:T(8,128)}), f32[256,9,768]{2,1,0:T(8,128)}) %all-gather.3.cloned.1.call-update) | async-done | bytes 7077904 | tf_op jit(solution)/shard_map/all_gather | solution.py:62
  453.1 9.8 %reshape.148 = f32[2304,768]{1,0:T(8,128)} reshape(f32[256,9,768]{2,1,0:T(8,128)} %all-gather.3.cloned.1.call-done) | data formatting | bytes 14155776
  462.8 5.5 %fusion.4 = f32[768,24]{0,1:T(8,128)S(1)} fusion(f32[2304,768]{1,0:T(8,128)} %reshape.148, s32[24]{0:T(128)S(1)} %dynamic-slice_reduce_fusion), kind=kOutput, calls=%fused_computation.21 | convolution fusion | flops 509663232 | bytes 7151712 | tf_op jit(solution)/shard_map/dot_general | solution.py:63
  468.3 3.1 multiply_convert_fusion
  473.3 2.0 gather_fusion.4
  475.7 4.1 collective-permute-start.4
  480.1 2.0 gather_fusion.5
  483.1 13.5 %collective-permute-done.4 = bf16[768,512]{1,0:T(8,128)(2,1)S(1)} collective-permute-done((bf16[768,512]{1,0:T(8,128)(2,1)S(1)}, bf16[768,512]{1,0:T(8,128)(2,1)S(1)}, u32[]{:S(2)}, u32[]{:S(2)}) %collective-permute-start.4) | collective-permute-done | bytes 786464 | tf_op jit(solution)/shard_map/ppermute | solution.py:13
  496.6 3.1 fusion.2
  (57 shorter events, 9.9 us)
Async XLA Ops:
  6.5 316.4 %copy-start = (f32[9,2304]{1,0:T(8,128)S(1)}, f32[9,2304]{1,0:T(8,128)}, u32[]{:S(2)}) copy-start(f32[9,2304]{1,0:T(8,128)} %param.17) | copy-start | bytes 248836
  6.5 316.4 %all-reduce.2.cloned.1.call-start = ((), (), s32[]{:S(2)}) async-start(), calls=%async_computation | async-start | bytes 14155776 | tf_op jit(solution)/shard_map/psum | solution.py:60
  7.3 11.3 %collective-permute-start = (bf16[512]{0:T(512)(128)(2,1)S(1)}, bf16[512]{0:T(512)(128)(2,1)S(1)}, u32[]{:S(2)}, u32[]{:S(2)}) collective-permute-start(bf16[512]{0:T(512)(128)(2,1)S(1)} %get-tuple-element.6), channel_id=1, source_target_pairs={{0,8},{8,16},{16,24},{24,32},{32,40},{40,48},{48,56},{56,64},{64,7... | collective-permute-start | bytes 3080 | tf_op jit(solution)/shard_map/ppermute | solution.py:13
  9.8 12.3 %collective-permute-start.1 = (bf16[512]{0:T(512)(128)(2,1)S(1)}, bf16[512]{0:T(512)(128)(2,1)S(1)}, u32[]{:S(2)}, u32[]{:S(2)}) collective-permute-start(bf16[512]{0:T(512)(128)(2,1)S(1)} %get-tuple-element.8), channel_id=1, source_target_pairs={{0,1},{1,2},{2,3},{3,4},{4,5},{5,6},{6,7},{7,0},{8,9},{9,10},{10,1... | collective-permute-start | bytes 3080 | tf_op jit(solution)/shard_map/ppermute | solution.py:13
  14.3 22.7 %collective-permute-start.2 = (bf16[768,512]{1,0:T(8,128)(2,1)S(1)}, bf16[768,512]{1,0:T(8,128)(2,1)S(1)}, u32[]{:S(2)}, u32[]{:S(2)}) collective-permute-start(bf16[768,512]{1,0:T(8,128)(2,1)S(1)} %get-tuple-element.15), channel_id=1, source_target_pairs={{0,8},{8,16},{16,24},{24,32},{32,40},{40,48},{48,56},{56,64},{64,7... | collective-permute-start | bytes 2359304 | tf_op jit(solution)/shard_map/ppermute | solution.py:13
  16.0 23.7 %collective-permute-start.3 = (bf16[768,512]{1,0:T(8,128)(2,1)}, bf16[768,512]{1,0:T(8,128)(2,1)S(1)}, u32[]{:S(2)}, u32[]{:S(2)}) collective-permute-start(bf16[768,512]{1,0:T(8,128)(2,1)} %get-tuple-element.16), channel_id=1, source_target_pairs={{0,1},{1,2},{2,3},{3,4},{4,5},{5,6},{6,7},{7,0},{8,9},{9,10},{10,1... | collective-permute-start | bytes 2359304 | tf_op jit(solution)/shard_map/ppermute | solution.py:13
  39.9 2.5 copy-start.5
  49.8 281.8 %copy-start.6 = (s32[1,2,512]{2,1,0:T(2,128)S(1)}, s32[1,2,512]{2,1,0:T(2,128)}, u32[]{:S(2)}) copy-start(s32[1,2,512]{2,1,0:T(2,128)} %param.13) | copy-start | bytes 12292
  49.8 287.0 %copy-start.4 = (bf16[1,768,1024]{2,1,0:T(8,128)(2,1)S(1)}, bf16[1,768,1024]{2,1,0:T(8,128)(2,1)}, u32[]{:S(2)}) copy-start(bf16[1,768,1024]{2,1,0:T(8,128)(2,1)} %param.11) | copy-start | bytes 4718596
  49.8 403.2 %all-gather.3.cloned.1.call-start = ((), (), s32[]{:S(2)}) async-start(), calls=%async_computation.1 | async-start | bytes 12632064 | tf_op jit(solution)/shard_map/all_gather | solution.py:62
  462.8 5.5 %copy-start.3 = (f32[768,2048]{1,0:T(8,128)S(1)}, f32[768,2048]{1,0:T(8,128)}, u32[]{:S(2)}) copy-start(f32[768,2048]{1,0:T(8,128)} %fusion) | copy-start | bytes 18874372
  471.4 1.6 copy-start.2
  475.7 20.8 %collective-permute-start.4 = (bf16[768,512]{1,0:T(8,128)(2,1)S(1)}, bf16[768,512]{1,0:T(8,128)(2,1)S(1)}, u32[]{:S(2)}, u32[]{:S(2)}) collective-permute-start(bf16[768,512]{1,0:T(8,128)(2,1)S(1)} %select_bitcast_fusion.1), channel_id=1, source_target_pairs={{0,248},{8,0},{16,8},{24,16},{32,24},{40,32},{48,40},{56,48},{64,5... | collective-permute-start | bytes 2359304 | tf_op jit(solution)/shard_map/ppermute | solution.py:13
  479.9 19.8 %copy-start.1 = (f32[9,2304]{1,0:T(8,128)S(1)}, f32[9,2304]{1,0:T(8,128)}, u32[]{:S(2)}) copy-start(f32[9,2304]{1,0:T(8,128)} %param.17) | copy-start | bytes 248836
  482.5 14.0 %collective-permute-start.5 = (bf16[768,512]{1,0:T(8,128)(2,1)S(1)}, bf16[768,512]{1,0:T(8,128)(2,1)S(1)}, u32[]{:S(2)}, u32[]{:S(2)}) collective-permute-start(bf16[768,512]{1,0:T(8,128)(2,1)S(1)} %select_bitcast_fusion), channel_id=1, source_target_pairs={{0,7},{1,0},{2,1},{3,2},{4,3},{5,4},{6,5},{7,6},{8,15},{9,8},{10,9... | collective-permute-start | bytes 2359304 | tf_op jit(solution)/shard_map/ppermute | solution.py:13
Sparse Core Ops, SparseCore 0:
  50.0 272.9 all-reduce.1
  331.7 121.2 all-gather.2
where the time goes:
time: 507 us
  waiting for transfers between devices  403 us (79%)
  local copies, waits for them, and re-layouts  38.6 us (8%)
  matrix products  35.3 us (7%)
  between operations  13.7 us (3%)
  starting transfers between devices  11.3 us (2%)
    psum x1, waiting for transfers between devices, on_device(): coarse_rhs = lax.psum(partial_rhs, ('wide', 'narrow'))  273 us
    all_gather x1, waiting for transfers between devices, on_device(): lax.all_gather(own_rows, ('wide', 'narrow'), axis=1, tiled=True)  106 us
    ppermute x6, waiting for transfers between devices, from_behind(): lax.ppermute(array, axis, [(i, (i + by) % devices) for i in range(devices)])  24.8 us
    ppermute x6, starting transfers between devices, from_behind(): lax.ppermute(array, axis, [(i, (i + by) % devices) for i in range(devices)])  11.3 us
    unnamed x15, local copies, waits for them, and re-layouts  11.3 us
    dot_general x1, matrix products, on_device(): local = jnp.dot(gathered, inverse, preferred_element_type=jnp.float32)  10.7 us
  transfers between devices with their start and end apart: 8, of which 4 were waited for; matrix products, arithmetic and copies ran while one was open for 6% of the time, Pallas kernels for 0%

commit v1 on v0

v1 whole, which is shorter than its diff:
```python
import jax
import jax.numpy as jnp
from jax import lax
from jax.experimental import pallas as pl
from jax.experimental.pallas import tpu as pltpu
from jax.sharding import PartitionSpec as P

BF = jnp.bfloat16
F32 = jnp.float32
NX = 4
NZ = 8
NY = 4
NCORE = 2
NARROW = NY * NCORE
WIDE = NX * NZ
WIDE_AXES = ("x", "z")
NARROW_AXES = ("y", "core")
LANES = 128
SLOT = 32
NT = (((1,), (1,)), ((), ()))
MIB = 1024 * 1024


def permute(array, axes, target):
    count = lax.axis_size(axes)
    return lax.ppermute(array, axes, [(i, target(i)) for i in range(count)])


def shift(array, axes, by):
    count = lax.axis_size(axes)
    return permute(array, axes, lambda i: (i + by) % count)


def exchange(array, bit):
    return permute(array, "z", lambda i: i ^ bit)


def whole(shape):
    return pl.BlockSpec(shape, lambda *_: (0,) * len(shape))


def params(mib=8):
    return pltpu.CompilerParams(vmem_limit_bytes=mib * MIB)


def after(array, *others):
    return lax.optimization_barrier((array, *others))[0]


def one_hot(row, count):
    lanes = row.shape[1]
    return jnp.where(lax.broadcasted_iota(jnp.int32, (count, lanes), 0) == row, 1.0, 0.0).astype(BF)


def dot_nt(a, b):
    return lax.dot_general(a, b, NT, preferred_element_type=F32)


def padded(basis):
    fill = jnp.zeros((SLOT - basis.shape[0], basis.shape[1]), F32)
    return jnp.concatenate([basis.astype(F32), fill], axis=0).astype(BF)


def cost(flops, moved):
    return pl.CostEstimate(flops=flops, bytes_accessed=moved, transcendentals=0)


def fetch(pairs, sems):
    copies = [pltpu.make_async_copy(src, dst, sems.at[i]) for i, (src, dst) in enumerate(pairs)]
    for copy in copies:
        copy.start()
    return copies


IN_HBM = pl.BlockSpec(memory_space=pltpu.HBM)


def first_kernel(
    basis_hbm, orient_hbm, coarse_hbm, wide_ref, narrow_ref, lines_ref, basis_ref, orient_ref, coarse_ref, strided, sems
):
    copies = fetch(((basis_hbm, basis_ref), (orient_hbm, orient_ref), (coarse_hbm, coarse_ref)), sems)
    copies[0].wait()
    copies[1].wait()
    face = orient_ref.shape[1]
    for row, out in ((0, wide_ref), (1, narrow_ref)):
        order = one_hot(orient_ref[row : row + 1, :], face)
        part = padded(basis_ref[:, (2 + row) * face : (3 + row) * face])
        out[...] = dot_nt(part, order).astype(BF)
    held, coarse = coarse_ref.shape
    blocks = coarse // LANES
    strided[...] = jnp.zeros_like(strided)
    copies[2].wait()
    for b in range(blocks):
        strided[pl.ds(b, held, stride=blocks), :] = coarse_ref[:, b * LANES : (b + 1) * LANES]
    lines_ref[...] = strided[: lines_ref.shape[0]].astype(BF)


def line_count(held, coarse):
    return -(-held * coarse // LANES // 16) * 16


def first(basis, orient, coarse_inverse):
    face = orient.shape[1]
    shape = jax.ShapeDtypeStruct((SLOT, face), BF)
    lines = (line_count(*coarse_inverse.shape), LANES)
    inputs = (basis, orient, coarse_inverse)
    return pl.pallas_call(
        first_kernel,
        in_specs=[IN_HBM] * len(inputs),
        out_shape=[shape, shape, jax.ShapeDtypeStruct(lines, BF)],
        scratch_shapes=[pltpu.VMEM(a.shape, a.dtype) for a in inputs]
        + [pltpu.VMEM((2 * lines[0], LANES), F32), pltpu.SemaphoreType.DMA((len(inputs),))],
        compiler_params=params(60),
    )(*inputs)


def outgoing_kernel(res_ref, share_ref, face_wide_ref, face_narrow_ref):
    face = face_wide_ref.shape[1]
    given = res_ref[...].astype(F32) * (1.0 - share_ref[...].astype(F32))
    face_wide_ref[...] = given[:, :face].astype(BF)
    face_narrow_ref[...] = given[:, face:].astype(BF)


def outgoing(res, share):
    rows, owned_count = res.shape
    face = owned_count // 2
    block = rows // 3
    half = jax.ShapeDtypeStruct((rows, face), BF)
    by_rows = lambda i: (i, 0)
    return pl.pallas_call(
        outgoing_kernel,
        grid=(3,),
        in_specs=[pl.BlockSpec((block, owned_count), by_rows), whole(share.shape)],
        out_specs=[pl.BlockSpec((block, face), by_rows)] * 2,
        out_shape=[half, half],
        compiler_params=params(),
        cost_estimate=cost(2 * res.size, 4 * res.size),
    )(res, share)


def stacked_bases(own_ref, wide_ref, narrow_ref):
    face = wide_ref.shape[1]
    zero = jnp.zeros((SLOT, face), BF)
    zeros = jnp.zeros((SLOT, 2 * face), BF)
    mine = jnp.concatenate([padded(own_ref[:, : 2 * face]), zeros, zeros, zeros], axis=0)
    theirs = jnp.concatenate(
        [
            zeros,
            jnp.concatenate([wide_ref[...], zero], axis=1),
            jnp.concatenate([zero, narrow_ref[...]], axis=1),
            zeros,
        ],
        axis=0,
    )
    return mine, theirs


def primal_kernel(res_ref, share_ref, own_ref, wide_ref, narrow_ref, out_ref):
    mine, theirs = stacked_bases(own_ref, wide_ref, narrow_ref)
    res = res_ref[...].astype(F32)
    shr = share_ref[...].astype(F32)
    kept = (res * shr).astype(BF)
    given = (res * (1.0 - shr)).astype(BF)
    out_ref[...] = (dot_nt(kept, mine) + dot_nt(given, theirs)).astype(BF)


def primal_parts(res, share, basis, basis_wide, basis_narrow):
    rows, owned_count = res.shape
    block = rows // 3
    return pl.pallas_call(
        primal_kernel,
        grid=(3,),
        in_specs=[
            pl.BlockSpec((block, owned_count), lambda i: (i, 0)),
            whole(share.shape),
            whole(basis.shape),
            whole(basis_wide.shape),
            whole(basis_narrow.shape),
        ],
        out_specs=pl.BlockSpec((block, LANES), lambda i: (i, 0)),
        out_shape=jax.ShapeDtypeStruct((rows, LANES), BF),
        compiler_params=params(16),
        cost_estimate=cost(4 * res.size * LANES, 2 * res.size),
    )(res, share, basis, basis_wide, basis_narrow)


def scatter_kernel(blocks, x_ref, high_ref, low_ref, out_ref, masked):
    rows = x_ref.shape[1]
    masked[...] = jnp.zeros_like(masked)
    total = jnp.zeros((blocks * SLOT, LANES), F32)
    for pair in range(x_ref.shape[0] // 2):
        x = jnp.concatenate([x_ref[2 * pair], x_ref[2 * pair + 1]], axis=1).astype(F32)
        high = jnp.concatenate([high_ref[2 * pair : 2 * pair + 1], high_ref[2 * pair + 1 : 2 * pair + 2]], axis=1)
        low = jnp.concatenate([low_ref[2 * pair : 2 * pair + 1], low_ref[2 * pair + 1 : 2 * pair + 2]], axis=1)
        x = jnp.concatenate([x, jnp.zeros((SLOT - rows, x.shape[1]), F32)], axis=0)
        for b in range(blocks):
            masked[b * SLOT : (b + 1) * SLOT] = jnp.where(high == b, x, 0.0).astype(BF)
        total += dot_nt(masked[...], one_hot(low, LANES))
    for b in range(blocks):
        out_ref[b] = total[b * SLOT : b * SLOT + rows].astype(BF)


def scatter(x, high, low, blocks):
    _, rows, _ = x.shape
    return pl.pallas_call(
        lambda *refs: scatter_kernel(blocks, *refs),
        out_shape=jax.ShapeDtypeStruct((blocks, rows, LANES), BF),
        scratch_shapes=[pltpu.VMEM((blocks * SLOT, 2 * LANES), BF)],
        compiler_params=params(),
    )(x, high, low)


def solve_kernel(parts_ref, *refs):
    *line_refs, out_ref, strided, inverse = refs
    parts, blocks, rows, _ = parts_ref.shape
    count = line_refs[0].shape[0]
    size = count // NZ
    strided[count:] = jnp.zeros((strided.shape[0] - count, LANES), F32)
    for x, ref in enumerate(line_refs):
        strided[:count] = ref[...].astype(F32)
        for z in range(NZ):
            at = x * LANES + z * 16
            for b in range(blocks):
                found = strided[pl.ds(z * size + b, 16, stride=blocks), :]
                inverse[at : at + 16, b * LANES : (b + 1) * LANES] = found.astype(BF)
    total = jnp.concatenate([sum(parts_ref[p, b].astype(F32) for p in range(parts)) for b in range(blocks)], axis=1)
    top = total.astype(BF)
    rest = (total - top.astype(F32)).astype(BF)
    both = jnp.concatenate([top.astype(F32), rest.astype(F32)], axis=0).astype(BF)
    product = dot_nt(both, inverse[...])
    product = (product[:rows] + product[rows:]).astype(BF)
    for p in range(NX):
        for n in range(out_ref.shape[0]):
            out_ref[n, p] = product[:, p * LANES : (p + 1) * LANES]


def solve(parts, lines):
    _, blocks, rows, _ = parts.shape
    spare = 16 * blocks
    return pl.pallas_call(
        solve_kernel,
        out_shape=jax.ShapeDtypeStruct((NARROW, NX, rows, LANES), BF),
        scratch_shapes=[
            pltpu.VMEM((lines[0].shape[0] + spare, LANES), F32),
            pltpu.VMEM((NX * LANES, blocks * LANES), BF),
        ],
        compiler_params=params(16),
    )(parts, *lines)


def gather_kernel(rows, corr_ref, high_ref, low_ref, out_ref):
    blocks = corr_ref.shape[0] // rows
    for pair in range(out_ref.shape[0] // 2):
        high = jnp.concatenate([high_ref[2 * pair : 2 * pair + 1], high_ref[2 * pair + 1 : 2 * pair + 2]], axis=1)
        low = jnp.concatenate([low_ref[2 * pair : 2 * pair + 1], low_ref[2 * pair + 1 : 2 * pair + 2]], axis=1)
        found = jnp.dot(corr_ref[...], one_hot(low, LANES), preferred_element_type=F32)
        total = jnp.zeros((rows, 2 * LANES), F32)
        for b in range(blocks):
            total = jnp.where(high == b, found[b * rows : (b + 1) * rows], total)
        out_ref[2 * pair] = total[:, :LANES].astype(BF)
        out_ref[2 * pair + 1] = total[:, LANES:].astype(BF)


def gather(corr, high, low, rows):
    return pl.pallas_call(
        lambda *refs: gather_kernel(rows, *refs),
        out_shape=jax.ShapeDtypeStruct((high.shape[0], rows, LANES), BF),
        compiler_params=params(),
    )(corr, high, low)


def column_copies(inverse_hbm, inverse, sems, first_column):
    count, rows, width = inverse.shape
    return [
        pltpu.make_async_copy(
            inverse_hbm.at[pl.ds(0, rows), pl.ds((first_column + i) * width, width)], inverse.at[i], sems.at[i]
        )
        for i in range(count)
    ]


def faces_kernel(
    res_ref, share_ref, got_wide_ref, got_narrow_ref, orient_ref, inverse_hbm, gathered_ref, wide_ref, narrow_ref, inverse, sems
):
    face = orient_ref.shape[1]
    copies = column_copies(inverse_hbm, inverse, sems, 2)
    for copy in copies:
        copy.start()
    gathered_ref[:, : 2 * face] = (res_ref[...].astype(F32) * share_ref[...].astype(F32)).astype(BF)
    orders = [one_hot(orient_ref[row : row + 1, :], face) for row in (0, 1)]
    for row, ref in ((0, got_wide_ref), (1, got_narrow_ref)):
        found = jnp.dot(ref[...], orders[row], preferred_element_type=F32)
        gathered_ref[:, (2 + row) * face : (3 + row) * face] = found.astype(BF)
    for row, ref in ((0, wide_ref), (1, narrow_ref)):
        copies[row].wait()
        product = jnp.dot(gathered_ref[...], inverse[row], preferred_element_type=F32).astype(BF)
        ref[...] = dot_nt(product, orders[row]).astype(BF)


def faces(res, share, got_wide, got_narrow, orient, inverse):
    rows = res.shape[0]
    face = orient.shape[1]
    unknowns = inverse.shape[0]
    half = jax.ShapeDtypeStruct((rows, face), BF)
    inputs = (res, share, got_wide, got_narrow, orient)
    return pl.pallas_call(
        faces_kernel,
        in_specs=[pl.BlockSpec(memory_space=pltpu.VMEM)] * len(inputs) + [IN_HBM],
        out_shape=[jax.ShapeDtypeStruct((rows, unknowns), BF), half, half],
        scratch_shapes=[pltpu.VMEM((2, unknowns, face), BF), pltpu.SemaphoreType.DMA((2,))],
        compiler_params=params(56),
        cost_estimate=cost(4 * rows * face * unknowns + 8 * rows * face * face, 4 * face * unknowns + 8 * rows * face),
    )(*inputs, inverse)


def owned_kernel(gathered_ref, inverse_hbm, out_ref, inverse, sems):
    copies = column_copies(inverse_hbm, inverse, sems, 0)
    face = inverse.shape[2]
    for copy in copies:
        copy.start()
    for i, copy in enumerate(copies):
        copy.wait()
        product = jnp.dot(gathered_ref[...], inverse[i], preferred_element_type=F32)
        out_ref[:, i * face : (i + 1) * face] = product.astype(BF)


def owned(gathered, inverse, face):
    rows, unknowns = gathered.shape
    return pl.pallas_call(
        owned_kernel,
        in_specs=[pl.BlockSpec(memory_space=pltpu.VMEM), IN_HBM],
        out_shape=jax.ShapeDtypeStruct((rows, 2 * face), BF),
        scratch_shapes=[pltpu.VMEM((2, unknowns, face), BF), pltpu.SemaphoreType.DMA((2,))],
        compiler_params=params(56),
        cost_estimate=cost(4 * rows * face * unknowns, 4 * face * unknowns + 4 * rows * unknowns),
    )(gathered, inverse)


def final_kernel(local_ref, back_wide_ref, back_narrow_ref, corr_ref, share_ref, own_ref, wide_ref, narrow_ref, out_ref):
    mine, theirs = stacked_bases(own_ref, wide_ref, narrow_ref)
    shr = share_ref[...].astype(F32)
    corr = corr_ref[...]
    kept = local_ref[...].astype(F32) + jnp.dot(corr, mine, preferred_element_type=F32)
    back = jnp.concatenate([back_wide_ref[...], back_narrow_ref[...]], axis=1).astype(F32)
    back = back + jnp.dot(corr, theirs, preferred_element_type=F32)
    out_ref[0] = (shr * kept + (1.0 - shr) * back).astype(BF)


def final(local, back_wide, back_narrow, corr, share, basis, basis_wide, basis_narrow):
    rows, owned_count = local.shape
    face = owned_count // 2
    block = rows // 3
    by_rows = lambda i: (i, 0)
    return pl.pallas_call(
        final_kernel,
        grid=(3,),
        in_specs=[
            pl.BlockSpec((block, owned_count), by_rows),
            pl.BlockSpec((block, face), by_rows),
            pl.BlockSpec((block, face), by_rows),
            pl.BlockSpec((block, LANES), by_rows),
            whole(share.shape),
            whole(basis.shape),
            whole(basis_wide.shape),
            whole(basis_narrow.shape),
        ],
        out_specs=pl.BlockSpec((1, block, owned_count), lambda i: (0, i, 0)),
        out_shape=jax.ShapeDtypeStruct((1, rows, owned_count), BF),
        compiler_params=params(12),
    )(local, back_wide, back_narrow, corr, share, basis, basis_wide, basis_narrow)


def patch_columns(primal_index):
    narrow = lax.axis_index(NARROW_AXES)
    count = primal_index.shape[1]
    grid = primal_index.reshape(WIDE, NARROW, count)
    grid = jnp.pad(grid, ((0, 0), (0, 0), (0, SLOT - count)), constant_values=-1)
    own = lax.dynamic_index_in_dim(grid, narrow, 1, keepdims=False)
    beside = lax.dynamic_index_in_dim(grid, (narrow + 1) % NARROW, 1, keepdims=False)
    empty = jnp.full((WIDE, LANES - 3 * SLOT), -1, jnp.int32)
    return jnp.concatenate([own, jnp.roll(own, -1, axis=0), beside, empty], axis=1)


def held_place(columns, held):
    owner, row = columns // held, columns % held
    w, n = owner // NARROW, owner % NARROW
    by_x = (lax.axis_index("x") - w // NZ) % NX
    apart = (lax.axis_index("z") ^ w) % NZ
    by_z = apart // 4 + (apart // 2) % 2 * 2 + apart % 2 * 4
    return jnp.where(columns < 0, -1, n * NX + by_x), by_z * 16 + row


def on_device(residual, share, orient, local_inverse, primal_basis, primal_index, coarse_inverse):
    res = residual[0]
    ori = orient[0]
    inverse = local_inverse[0]
    basis = primal_basis[0]
    rows = res.shape[0]
    held, coarse = coarse_inverse.shape
    chunk = rows // WIDE

    mine_wide, mine_narrow, lines = first(basis, ori, coarse_inverse)
    basis_wide = shift(mine_wide, WIDE_AXES, -1)
    basis_narrow = shift(mine_narrow, NARROW_AXES, -1)
    other = exchange(lines, 4)

    face_wide, face_narrow = outgoing(after(res, mine_wide), share)
    got_wide = shift(face_wide, WIDE_AXES, 1)
    got_narrow = shift(face_narrow, NARROW_AXES, 1)

    primal = primal_parts(after(res, face_wide), share, basis, basis_wide, basis_narrow)
    lines = jnp.concatenate([after(lines, primal), other], axis=0)
    other = exchange(lines, 2)
    chunks = lax.all_to_all(after(primal, lines).reshape(WIDE, chunk, LANES), WIDE_AXES, 0, 0)

    columns = patch_columns(after(primal_index, primal))
    high, low = columns >> 7, columns & 127
    high_held, low_held = held_place(columns, held)

    lines = jnp.concatenate([after(lines, high, high_held), other], axis=0)
    lines = jnp.concatenate([lines, exchange(lines, 1)], axis=0)
    pieces = [lines] + [shift(lines, "x", k) for k in range(1, NX)]

    partial = scatter(after(chunks, lines), high, low, coarse // LANES)
    parts = lax.all_gather(partial, NARROW_AXES)
    corr = solve(parts, pieces)

    gathered, send_wide, send_narrow = faces(res, share, after(got_wide, corr), got_narrow, ori, inverse)
    corr = lax.all_to_all(corr, NARROW_AXES, 0, 0)
    back_wide = shift(after(send_wide, corr), WIDE_AXES, -1)
    back_narrow = shift(after(send_narrow, corr), NARROW_AXES, -1)
    corr = gather(after(corr, send_wide).reshape(-1, LANES), high_held, low_held, chunk)
    local = owned(after(gathered, corr), inverse, face_wide.shape[1])
    corr = lax.all_to_all(corr, WIDE_AXES, 0, 0).reshape(rows, LANES)

    return final(local, back_wide, back_narrow, corr, share, basis, basis_wide, basis_narrow)


def solution(mesh):
    grid = jax.sharding.Mesh(mesh.devices.reshape(NX, NZ, NY, NCORE), WIDE_AXES + NARROW_AXES)
    patches = WIDE_AXES + NARROW_AXES
    placed = (
        P(patches, None, None),
        P(patches, None),
        P(patches, None, None),
        P(patches, None, None),
        P(patches, None, None),
        P(),
        P(patches, None),
    )
    return jax.shard_map(
        on_device,
        mesh=grid,
        in_specs=placed,
        out_specs=P(patches, None, None),
        check_vma=False,
    )
```

time: 507 us -> 115 us (0.23)
  waiting for transfers between devices: 403 us -> 19.1 us
  matrix products: 35.3 us -> 0 us
  local copies, waits for them, and re-layouts: 38.6 us -> 3.82 us
  Pallas kernels: 0 us -> 31 us
  starting transfers between devices: 11.3 us -> 41 us
  blocking collectives: 0 us -> 17.8 us
  between operations: 13.7 us -> 0.2 us
    psum x1 -> x0, waiting for transfers between devices: 273 us -> none  [on_device(): coarse_rhs = lax.psum(partial_rhs, ('wide', 'narrow'))]
    all_gather x1 -> x0, waiting for transfers between devices: 106 us -> none  [on_device(): lax.all_gather(own_rows, ('wide', 'narrow'), axis=1, tiled=True)]
    dot_general x6 -> x0, matrix products: 35.3 us -> none  [the longest x1 10.7 us: on_device(): local = jnp.dot(gathered, inverse, preferred_element_type=jnp.float32)]
    pallas_call x0 -> x9, Pallas kernels: none -> 31 us  [the longest x1 8.76 us: faces(): pl.pallas_call(faces_kernel, in_specs=[pl.BlockSpec(memory_space=pltpu.VM...]
    all_to_all x0 -> x3, starting transfers between devices: none -> 21.1 us  [the longest x1 8.42 us: on_device(): corr = lax.all_to_all(corr, WIDE_AXES, 0, 0).reshape(rows, LANES)]
    all_gather x0 -> x1, blocking collectives: none -> 17.8 us  [on_device(): parts = lax.all_gather(partial, NARROW_AXES)]
    gather x10 -> x0, local copies, waits for them, and re-layouts: 16.2 us -> none  [the longest x1 3.51 us: on_device(): wt_wide = jnp.take(shr_wide, ori[0]).astype(jnp.float32)]
    ppermute x6 -> x12, waiting for transfers between devices: 24.8 us -> 13.4 us  [permute(): return lax.ppermute(array, axes, [(i, target(i)) for i in range(count)])]
  transfers between devices with their start and end apart: 8 -> 15, of which waited for: 4 -> 3; matrix products, arithmetic and copies ran while one was open for 6% -> 0% of each run, Pallas kernels for 0% -> 23%
where the time goes in v1:
time: 115 us; the launch traced here: 113 us
  starting transfers between devices  41 us (36%)
  Pallas kernels  31 us (27%)
  waiting for transfers between devices  19.1 us (17%)
  blocking collectives  17.8 us (15%)
  local copies, waits for them, and re-layouts  3.82 us (3%)
    ppermute x12, starting transfers between devices, permute(): return lax.ppermute(array, axes, [(i, target(i)) for i in range(count)])  19.9 us
    all_gather x1, blocking collectives, on_device(): parts = lax.all_gather(partial, NARROW_AXES)  17.8 us
    ppermute x12, waiting for transfers between devices, permute(): return lax.ppermute(array, axes, [(i, target(i)) for i in range(count)])  13.4 us
    pallas_call x1, Pallas kernels, faces(): pl.pallas_call(faces_kernel, in_specs=[pl.BlockSpec(memory_space=pltpu.VM...  8.76 us
    all_to_all x1, starting transfers between devices, on_device(): corr = lax.all_to_all(corr, WIDE_AXES, 0, 0).reshape(rows, LANES)  8.42 us
    pallas_call x1, Pallas kernels, owned(): pl.pallas_call(owned_kernel, in_specs=[pl.BlockSpec(memory_space=pltpu.VM...  8.22 us
    all_to_all x1, starting transfers between devices, on_device(): lax.all_to_all(after(primal, lines).reshape(WIDE, chunk, LANES), WIDE_AXE...  6.7 us
    all_to_all x1, starting transfers between devices, on_device(): corr = lax.all_to_all(corr, NARROW_AXES, 0, 0)  5.99 us
  transfers between devices with their start and end apart: 15, of which 3 were waited for; matrix products, arithmetic and copies ran while one was open for 0% of the time, Pallas kernels for 23%

profile of v1, /device:TPU:1, one launch (start us, length us, event | category | flops | bytes accessed | tf_op | source)
XLA Modules:
  0.0 113.2 jit_solution(3619850975476197211)
XLA Ops:
  0.0 2.1 %shard_map.73 = (bf16[32,512]{1,0:T(8,128)(2,1)}, bf16[32,512]{1,0:T(8,128)(2,1)}, bf16[176,128]{1,0:T(8,128)(2,1)}) custom-call(bf16[24,2048]{1,0:T(8,128)(2,1)} %bitcast.21, s32[2,512]{1,0:T(2,128)} %bitcast.29, f32[9,2304]{1,0:T(8,128)} %coarse_hbm.1), custom_call_target="tpu_custom_call" | custom-call | tf_op jit(solution)/shard_map/pallas_call | solution.py:107
  2.1 3.3 %collective-permute-start.2 = (bf16[32,512]{1,0:T(8,128)(2,1)}, bf16[32,512]{1,0:T(8,128)(2,1)S(1)}, u32[]{:S(2)}, u32[]{:S(2)}) collective-permute-start(bf16[32,512]{1,0:T(8,128)(2,1)} %get-tuple-element.29), channel_id=1, source_target_pairs={{0,7},{1,0},{2,1},{3,2},{4,3},{5,4},{6,5},{7,6},{8,15},{9,8},{10,9... | collective-permute-start | bytes 98312 | tf_op jit(solution)/shard_map/ppermute | solution.py:26
  5.3 6.0 %collective-permute-start.1 = (bf16[32,512]{1,0:T(8,128)(2,1)}, bf16[32,512]{1,0:T(8,128)(2,1)S(1)}, u32[]{:S(2)}, u32[]{:S(2)}) collective-permute-start(bf16[32,512]{1,0:T(8,128)(2,1)} %get-tuple-element.25), channel_id=1, source_target_pairs={{0,248},{8,0},{16,8},{24,16},{32,24},{40,32},{48,40},{56,48},{64,5... | collective-permute-start | bytes 98312 | tf_op jit(solution)/shard_map/ppermute | solution.py:26
  11.4 1.4 %copy-done.1 = bf16[1,768,1024]{2,1,0:T(8,128)(2,1)S(1)} copy-done((bf16[1,768,1024]{2,1,0:T(8,128)(2,1)S(1)}, bf16[1,768,1024]{2,1,0:T(8,128)(2,1)}, u32[]{:S(2)}) %copy-start.1) | copy-done | bytes 1572888
  13.5 1.5 %shard_map.74 = (bf16[768,512]{1,0:T(8,128)(2,1)}, bf16[768,512]{1,0:T(8,128)(2,1)S(1)}) custom-call(bf16[768,1024]{1,0:T(8,128)(2,1)S(1)} %bitcast.18, bf16[1,1024]{1,0:T(2,128)(2,1)S(1)} %copy-done.4), custom_call_target="tpu_custom_call" | custom-call | flops 1572864 | bytes 3145728 | tf_op jit(solution)/shard_map/pallas_call | solution.py:130
  15.0 1.6 %collective-permute-start.9 = (bf16[768,512]{1,0:T(8,128)(2,1)S(1)}, bf16[768,512]{1,0:T(8,128)(2,1)}, u32[]{:S(2)}, u32[]{:S(2)}) collective-permute-start(bf16[768,512]{1,0:T(8,128)(2,1)S(1)} %get-tuple-element.37), channel_id=1, source_target_pairs={{0,1},{1,2},{2,3},{3,4},{4,5},{5,6},{6,7},{7,0},{8,9},{9,10},{10,1... | collective-permute-start | bytes 2359304 | tf_op jit(solution)/shard_map/ppermute | solution.py:26
  17.5 2.1 %shard_map.75 = bf16[768,128]{1,0:T(8,128)(2,1)} custom-call(bf16[768,1024]{1,0:T(8,128)(2,1)S(1)} %bitcast.19, bf16[1,1024]{1,0:T(2,128)(2,1)S(1)} %copy-done.5, bf16[24,2048]{1,0:T(8,128)(2,1)S(1)} %bitcast.22, bf16[32,512]{1,0:T(8,128)(2,1)S(1)} %collective-permute-done.1.wide_ref, bf16[32,512]{1,0:T(8,128)(2,1)S(1)} %collective-permute-done.2.narrow_ref), custom_call_target="tpu_custom_call" | custom-call | flops 402653184 | bytes 1572864 | tf_op jit(solution)/shard_map/pallas_call | solution.py:170
  21.4 6.7 %all-to-all-start = ((bf16[32,24,128]{2,1,0:T(8,128)(2,1)}), bf16[32,24,128]{2,1,0:T(8,128)(2,1)S(1)}, u32[]{:S(2)}, u32[]{:S(2)}) async-start(bf16[32,24,128]{2,1,0:T(8,128)(2,1)} %bitcast.3), calls=%async_computation | async-start | bytes 393216 | tf_op jit(solution)/shard_map/all_to_all | solution.py:414
  28.1 7.2 %collective-permute-done.4 = bf16[352,128]{1,0:T(8,128)(2,1)S(1)} collective-permute-done((bf16[352,128]{1,0:T(8,128)(2,1)S(1)}, bf16[352,128]{1,0:T(8,128)(2,1)S(1)}, u32[]{:S(2)}, u32[]{:S(2)}) %collective-permute-start.4) | collective-permute-done | bytes 90144 | tf_op jit(solution)/shard_map/ppermute | solution.py:26
  35.3 1.6 %collective-permute-start.5 = (bf16[704,128]{1,0:T(8,128)(2,1)S(1)}, bf16[704,128]{1,0:T(8,128)(2,1)S(1)}, u32[]{:S(2)}, u32[]{:S(2)}) collective-permute-start(bf16[704,128]{1,0:T(8,128)(2,1)S(1)} %pad_maximum_fusion), channel_id=1, source_target_pairs={{0,8},{8,0},{16,24},{24,16},{32,40},{40,32},{48,56},{56,48},{1,9},... | collective-permute-start | bytes 540680 | tf_op jit(solution)/shard_map/ppermute | solution.py:26
  37.0 6.1 %collective-permute-done.5 = bf16[704,128]{1,0:T(8,128)(2,1)S(1)} collective-permute-done((bf16[704,128]{1,0:T(8,128)(2,1)S(1)}, bf16[704,128]{1,0:T(8,128)(2,1)S(1)}, u32[]{:S(2)}, u32[]{:S(2)}) %collective-permute-start.5) | collective-permute-done | bytes 180256 | tf_op jit(solution)/shard_map/ppermute | solution.py:26
  43.1 2.6 %collective-permute-start.8 = (bf16[1408,128]{1,0:T(8,128)(2,1)S(1)}, bf16[1408,128]{1,0:T(8,128)(2,1)S(1)}, u32[]{:S(2)}, u32[]{:S(2)}) collective-permute-start(bf16[1408,128]{1,0:T(8,128)(2,1)S(1)} %constant_dynamic-update-slice_fusion.2.refs_0_), channel_id=1, source_target_pairs={{0,192},{64,0},{128,64},{192,128},{1,193},{65,1},{129,65},{193,129... | collective-permute-start | bytes 1081352 | tf_op jit(solution)/shard_map/ppermute | solution.py:26
  46.8 1.4 %shard_map.76 = bf16[18,24,128]{2,1,0:T(8,128)(2,1)S(1)} custom-call(bf16[32,24,128]{2,1,0:T(8,128)(2,1)S(1)} %all-to-all-done.refs_0_, s32[32,128]{1,0:T(8,128)S(1)} %get-tuple-element.51.refs_1_, s32[32,128]{1,0:T(8,128)S(1)} %get-tuple-element.49.refs_2_), custom_call_target="tpu_custom_call" | custom-call | tf_op jit(solution)/shard_map/pallas_call | solution.py:205
  48.2 17.8 %all-gather = bf16[144,24,128]{2,1,0:T(8,128)(2,1)S(1)} all-gather(bf16[18,24,128]{2,1,0:T(8,128)(2,1)S(1)} %shard_map.76), channel_id=2, replica_groups=mesh['x'=4,'z'=8,'y'=4,'core'=2] {'y','core'}, dimensions={0}, use_global_device_ids=true | all-gather | bytes 995328 | tf_op jit(solution)/shard_map/all_gather | solution.py:425
  66.0 1.9 %shard_map.77 = bf16[8,4,24,128]{3,2,1,0:T(8,128)(2,1)} custom-call(bf16[8,18,24,128]{3,2,1,0:T(8,128)(2,1)S(1)} %bitcast.20, bf16[1408,128]{1,0:T(8,128)(2,1)S(1)} %constant_dynamic-update-slice_fusion.2.refs_0_, bf16[1408,128]{1,0:T(8,128)(2,1)S(1)} %collective-permute-done.6.refs_1_, bf16[1408,128]{1,0:T(8,128)(2,1)S(1)} %collective-permute-done.7.refs_2_, ...), custom_call_target="tpu_custom_call" | custom-call | tf_op jit(solution)/shard_map/pallas_call | solution.py:240
  67.9 6.0 %all-to-all-start.1 = ((bf16[8,4,24,128]{3,2,1,0:T(8,128)(2,1)}), bf16[8,4,24,128]{3,2,1,0:T(8,128)(2,1)S(1)}, u32[]{:S(2)}, u32[]{:S(2)}) async-start(bf16[8,4,24,128]{3,2,1,0:T(8,128)(2,1)} %shard_map.77), calls=%async_computation.1 | async-start | bytes 393216 | tf_op jit(solution)/shard_map/all_to_all | solution.py:429
  73.9 8.8 %shard_map.78 = (bf16[768,2048]{1,0:T(8,128)(2,1)}, bf16[768,512]{1,0:T(8,128)(2,1)}, bf16[768,512]{1,0:T(8,128)(2,1)}) custom-call(bf16[768,1024]{1,0:T(8,128)(2,1)} %bitcast.17, bf16[1,1024]{1,0:T(2,128)(2,1)} %share_ref.7, bf16[768,512]{1,0:T(8,128)(2,1)} %collective-permute-done.got_wide_ref, bf16[768,512]{1,0:T(8,128)(2,1)} %collective-permute-done.9.got_narrow_ref, ...), custom_call_target="tpu_custom_call" | custom-call | flops 4831838208 | bytes 7340032 | tf_op jit(solution)/shard_map/pallas_call | solution.py:306
  82.7 1.3 %collective-permute-start.10 = (bf16[768,512]{1,0:T(8,128)(2,1)}, bf16[768,512]{1,0:T(8,128)(2,1)S(1)}, u32[]{:S(2)}, u32[]{:S(2)}) collective-permute-start(bf16[768,512]{1,0:T(8,128)(2,1)} %get-tuple-element.42), channel_id=1, source_target_pairs={{0,248},{8,0},{16,8},{24,16},{32,24},{40,32},{48,40},{56,48},{64,5... | collective-permute-start | bytes 2359304 | tf_op jit(solution)/shard_map/ppermute | solution.py:26
  84.3 2.5 %shard_map.79 = bf16[32,24,128]{2,1,0:T(8,128)(2,1)} custom-call(bf16[768,128]{1,0:T(8,128)(2,1)S(1)} %bitcast.25, s32[32,128]{1,0:T(8,128)S(1)} %get-tuple-element.50.refs_1_, s32[32,128]{1,0:T(8,128)S(1)} %get-tuple-element.45.refs_2_), custom_call_target="tpu_custom_call" | custom-call | tf_op jit(solution)/shard_map/pallas_call | solution.py:265
  86.8 8.4 %all-to-all-start.2 = ((bf16[32,24,128]{2,1,0:T(8,128)(2,1)}), bf16[32,24,128]{2,1,0:T(8,128)(2,1)S(1)}, u32[]{:S(2)}, u32[]{:S(2)}) async-start(bf16[32,24,128]{2,1,0:T(8,128)(2,1)} %shard_map.79), calls=%async_computation.2 | async-start | bytes 393216 | tf_op jit(solution)/shard_map/all_to_all | solution.py:434
  95.2 8.2 %shard_map.80.local_ref = bf16[768,1024]{1,0:T(8,128)(2,1)} custom-call(bf16[768,2048]{1,0:T(8,128)(2,1)} %get-tuple-element.41.gathered_ref, bf16[2048,2048]{1,0:T(8,128)(2,1)} %bitcast.27), custom_call_target="tpu_custom_call" | custom-call | flops 3221225472 | bytes 10485760 | tf_op jit(solution)/shard_map/pallas_call | solution.py:329
  103.5 5.8 %all-to-all-done.2 = bf16[32,24,128]{2,1,0:T(8,128)(2,1)S(1)} async-done(((bf16[32,24,128]{2,1,0:T(8,128)(2,1)}), bf16[32,24,128]{2,1,0:T(8,128)(2,1)S(1)}, u32[]{:S(2)}, u32[]{:S(2)}) %all-to-all-start.2) | async-done | bytes 196640 | tf_op jit(solution)/shard_map/all_to_all | solution.py:434
  109.3 1.4 %copy-done = bf16[768,1024]{1,0:T(8,128)(2,1)S(1)} copy-done((bf16[768,1024]{1,0:T(8,128)(2,1)S(1)}, bf16[768,1024]{1,0:T(8,128)(2,1)}, u32[]{:S(2)}) %copy-start) | copy-done | bytes 1572888
  110.7 2.5 %shard_map.81 = bf16[1,768,1024]{2,1,0:T(8,128)(2,1)} custom-call(bf16[768,1024]{1,0:T(8,128)(2,1)S(1)} %copy-done, bf16[768,512]{1,0:T(8,128)(2,1)S(1)} %collective-permute-done.10.back_wide_ref, bf16[768,512]{1,0:T(8,128)(2,1)S(1)} %collective-permute-done.11.back_narrow_ref, bf16[768,128]{1,0:T(8,128)(2,1)S(1)} %bitcast.24, ...), custom_call_target="tpu_custom_call" | custom-call | tf_op jit(solution)/shard_map/pallas_call | solution.py:354
  (49 shorter events, 4.9 us)
Async XLA Ops:
  0.0 17.5 %copy-start.3 = (bf16[1,24,2048]{2,1,0:T(8,128)(2,1)S(1)}, bf16[1,24,2048]{2,1,0:T(8,128)(2,1)}, u32[]{:S(2)}) copy-start(bf16[1,24,2048]{2,1,0:T(8,128)(2,1)} %param.11) | copy-start | bytes 294916
  0.0 17.5 %copy-start.5 = (bf16[1,1024]{1,0:T(2,128)(2,1)S(1)}, bf16[1,1024]{1,0:T(2,128)(2,1)}, u32[]{:S(2)}) copy-start(bf16[1,1024]{1,0:T(2,128)(2,1)} %share_ref.7) | copy-start | bytes 6148
  2.1 15.4 %collective-permute-start.2 = (bf16[32,512]{1,0:T(8,128)(2,1)}, bf16[32,512]{1,0:T(8,128)(2,1)S(1)}, u32[]{:S(2)}, u32[]{:S(2)}) collective-permute-start(bf16[32,512]{1,0:T(8,128)(2,1)} %get-tuple-element.29), channel_id=1, source_target_pairs={{0,7},{1,0},{2,1},{3,2},{4,3},{5,4},{6,5},{7,6},{8,15},{9,8},{10,9... | collective-permute-start | bytes 98312 | tf_op jit(solution)/shard_map/ppermute | solution.py:26
  5.3 12.2 %collective-permute-start.1 = (bf16[32,512]{1,0:T(8,128)(2,1)}, bf16[32,512]{1,0:T(8,128)(2,1)S(1)}, u32[]{:S(2)}, u32[]{:S(2)}) collective-permute-start(bf16[32,512]{1,0:T(8,128)(2,1)} %get-tuple-element.25), channel_id=1, source_target_pairs={{0,248},{8,0},{16,8},{24,16},{32,24},{40,32},{48,40},{56,48},{64,5... | collective-permute-start | bytes 98312 | tf_op jit(solution)/shard_map/ppermute | solution.py:26
  11.4 8.7 %collective-permute-start.3 = (bf16[176,128]{1,0:T(8,128)(2,1)}, bf16[176,128]{1,0:T(8,128)(2,1)S(1)}, u32[]{:S(2)}, u32[]{:S(2)}) collective-permute-start(bf16[176,128]{1,0:T(8,128)(2,1)} %get-tuple-element.31), channel_id=1, source_target_pairs={{0,32},{8,40},{16,48},{24,56},{32,0},{40,8},{48,16},{56,24},{1,33}... | collective-permute-start | bytes 135176 | tf_op jit(solution)/shard_map/ppermute | solution.py:26
  11.4 1.4 %copy-start.1 = (bf16[1,768,1024]{2,1,0:T(8,128)(2,1)S(1)}, bf16[1,768,1024]{2,1,0:T(8,128)(2,1)}, u32[]{:S(2)}) copy-start(bf16[1,768,1024]{2,1,0:T(8,128)(2,1)} %param.7) | copy-start | bytes 4718596
  12.8 0.7 copy-start.4
  13.5 4.0 %copy-start.2 = (bf16[1,768,1024]{2,1,0:T(8,128)(2,1)S(1)}, bf16[1,768,1024]{2,1,0:T(8,128)(2,1)}, u32[]{:S(2)}) copy-start(bf16[1,768,1024]{2,1,0:T(8,128)(2,1)} %param.7) | copy-start | bytes 4718596
  13.5 6.2 %copy-start.8 = (s32[256,24]{0,1:T(8,128)S(1)}, s32[256,24]{0,1:T(8,128)}, u32[]{:S(2)}) copy-start(s32[256,24]{0,1:T(8,128)} %param.12) | copy-start | bytes 73732
  15.0 5.0 %copy-start.7 = (bf16[176,128]{1,0:T(8,128)(2,1)S(1)}, bf16[176,128]{1,0:T(8,128)(2,1)}, u32[]{:S(2)}) copy-start(bf16[176,128]{1,0:T(8,128)(2,1)} %get-tuple-element.31) | copy-start | bytes 135172
  15.0 58.9 %collective-permute-start.9 = (bf16[768,512]{1,0:T(8,128)(2,1)S(1)}, bf16[768,512]{1,0:T(8,128)(2,1)}, u32[]{:S(2)}, u32[]{:S(2)}) collective-permute-start(bf16[768,512]{1,0:T(8,128)(2,1)S(1)} %get-tuple-element.37), channel_id=1, source_target_pairs={{0,1},{1,2},{2,3},{3,4},{4,5},{5,6},{6,7},{7,0},{8,9},{9,10},{10,1... | collective-permute-start | bytes 2359304 | tf_op jit(solution)/shard_map/ppermute | solution.py:26
  16.5 57.4 %collective-permute-start = (bf16[768,512]{1,0:T(8,128)(2,1)}, bf16[768,512]{1,0:T(8,128)(2,1)}, u32[]{:S(2)}, u32[]{:S(2)}) collective-permute-start(bf16[768,512]{1,0:T(8,128)(2,1)} %get-tuple-element.27), channel_id=1, source_target_pairs={{0,8},{8,16},{16,24},{24,32},{32,40},{40,48},{48,56},{56,64},{64,7... | collective-permute-start | bytes 2359304 | tf_op jit(solution)/shard_map/ppermute | solution.py:26
  20.1 15.3 %collective-permute-start.4 = (bf16[352,128]{1,0:T(8,128)(2,1)S(1)}, bf16[352,128]{1,0:T(8,128)(2,1)S(1)}, u32[]{:S(2)}, u32[]{:S(2)}) collective-permute-start(bf16[352,128]{1,0:T(8,128)(2,1)S(1)} %constant_dynamic-update-slice_fusion), channel_id=1, source_target_pairs={{0,16},{8,24},{16,0},{24,8},{32,48},{40,56},{48,32},{56,40},{1,17}... | collective-permute-start | bytes 270344 | tf_op jit(solution)/shard_map/ppermute | solution.py:26
  21.4 25.4 %all-to-all-start = ((bf16[32,24,128]{2,1,0:T(8,128)(2,1)}), bf16[32,24,128]{2,1,0:T(8,128)(2,1)S(1)}, u32[]{:S(2)}, u32[]{:S(2)}) async-start(bf16[32,24,128]{2,1,0:T(8,128)(2,1)} %bitcast.3), calls=%async_computation | async-start | bytes 393216 | tf_op jit(solution)/shard_map/all_to_all | solution.py:414
  35.3 7.7 %collective-permute-start.5 = (bf16[704,128]{1,0:T(8,128)(2,1)S(1)}, bf16[704,128]{1,0:T(8,128)(2,1)S(1)}, u32[]{:S(2)}, u32[]{:S(2)}) collective-permute-start(bf16[704,128]{1,0:T(8,128)(2,1)S(1)} %pad_maximum_fusion), channel_id=1, source_target_pairs={{0,8},{8,0},{16,24},{24,16},{32,40},{40,32},{48,56},{56,48},{1,9},... | collective-permute-start | bytes 540680 | tf_op jit(solution)/shard_map/ppermute | solution.py:26
  43.1 22.9 %collective-permute-start.8 = (bf16[1408,128]{1,0:T(8,128)(2,1)S(1)}, bf16[1408,128]{1,0:T(8,128)(2,1)S(1)}, u32[]{:S(2)}, u32[]{:S(2)}) collective-permute-start(bf16[1408,128]{1,0:T(8,128)(2,1)S(1)} %constant_dynamic-update-slice_fusion.2.refs_0_), channel_id=1, source_target_pairs={{0,192},{64,0},{128,64},{192,128},{1,193},{65,1},{129,65},{193,129... | collective-permute-start | bytes 1081352 | tf_op jit(solution)/shard_map/ppermute | solution.py:26
  45.6 20.3 %collective-permute-start.7 = (bf16[1408,128]{1,0:T(8,128)(2,1)S(1)}, bf16[1408,128]{1,0:T(8,128)(2,1)S(1)}, u32[]{:S(2)}, u32[]{:S(2)}) collective-permute-start(bf16[1408,128]{1,0:T(8,128)(2,1)S(1)} %constant_dynamic-update-slice_fusion.2.refs_0_), channel_id=1, source_target_pairs={{0,128},{64,192},{128,0},{192,64},{1,129},{65,193},{129,1},{193,65... | collective-permute-start | bytes 1081352 | tf_op jit(solution)/shard_map/ppermute | solution.py:26
  46.2 19.8 %collective-permute-start.6 = (bf16[1408,128]{1,0:T(8,128)(2,1)S(1)}, bf16[1408,128]{1,0:T(8,128)(2,1)S(1)}, u32[]{:S(2)}, u32[]{:S(2)}) collective-permute-start(bf16[1408,128]{1,0:T(8,128)(2,1)S(1)} %constant_dynamic-update-slice_fusion.2.refs_0_), channel_id=1, source_target_pairs={{0,64},{64,128},{128,192},{192,0},{1,65},{65,129},{129,193},{193,1... | collective-permute-start | bytes 1081352 | tf_op jit(solution)/shard_map/ppermute | solution.py:26
  67.9 14.8 %all-to-all-start.1 = ((bf16[8,4,24,128]{3,2,1,0:T(8,128)(2,1)}), bf16[8,4,24,128]{3,2,1,0:T(8,128)(2,1)S(1)}, u32[]{:S(2)}, u32[]{:S(2)}) async-start(bf16[8,4,24,128]{3,2,1,0:T(8,128)(2,1)} %shard_map.77), calls=%async_computation.1 | async-start | bytes 393216 | tf_op jit(solution)/shard_map/all_to_all | solution.py:429
  82.7 26.5 %collective-permute-start.10 = (bf16[768,512]{1,0:T(8,128)(2,1)}, bf16[768,512]{1,0:T(8,128)(2,1)S(1)}, u32[]{:S(2)}, u32[]{:S(2)}) collective-permute-start(bf16[768,512]{1,0:T(8,128)(2,1)} %get-tuple-element.42), channel_id=1, source_target_pairs={{0,248},{8,0},{16,8},{24,16},{32,24},{40,32},{48,40},{56,48},{64,5... | collective-permute-start | bytes 2359304 | tf_op jit(solution)/shard_map/ppermute | solution.py:26
  84.0 25.2 %collective-permute-start.11 = (bf16[768,512]{1,0:T(8,128)(2,1)}, bf16[768,512]{1,0:T(8,128)(2,1)S(1)}, u32[]{:S(2)}, u32[]{:S(2)}) collective-permute-start(bf16[768,512]{1,0:T(8,128)(2,1)} %get-tuple-element.44), channel_id=1, source_target_pairs={{0,7},{1,0},{2,1},{3,2},{4,3},{5,4},{6,5},{7,6},{8,15},{9,8},{10,9... | collective-permute-start | bytes 2359304 | tf_op jit(solution)/shard_map/ppermute | solution.py:26
  86.8 22.4 %all-to-all-start.2 = ((bf16[32,24,128]{2,1,0:T(8,128)(2,1)}), bf16[32,24,128]{2,1,0:T(8,128)(2,1)S(1)}, u32[]{:S(2)}, u32[]{:S(2)}) async-start(bf16[32,24,128]{2,1,0:T(8,128)(2,1)} %shard_map.79), calls=%async_computation.2 | async-start | bytes 393216 | tf_op jit(solution)/shard_map/all_to_all | solution.py:434
  95.2 14.0 %copy-start.6 = (bf16[1,1024]{1,0:T(2,128)(2,1)S(1)}, bf16[1,1024]{1,0:T(2,128)(2,1)}, u32[]{:S(2)}) copy-start(bf16[1,1024]{1,0:T(2,128)(2,1)} %share_ref.7) | copy-start | bytes 6148
  109.3 1.4 %copy-start = (bf16[768,1024]{1,0:T(8,128)(2,1)S(1)}, bf16[768,1024]{1,0:T(8,128)(2,1)}, u32[]{:S(2)}) copy-start(bf16[768,1024]{1,0:T(8,128)(2,1)} %shard_map.80.local_ref) | copy-start | bytes 4718596

commit v2 on v1

--- a/solution.py
+++ b/solution.py
@@ -75,41 +75,55 @@
 IN_HBM = pl.BlockSpec(memory_space=pltpu.HBM)
 
 
-def first_kernel(
-    basis_hbm, orient_hbm, coarse_hbm, wide_ref, narrow_ref, lines_ref, basis_ref, orient_ref, coarse_ref, strided, sems
-):
-    copies = fetch(((basis_hbm, basis_ref), (orient_hbm, orient_ref), (coarse_hbm, coarse_ref)), sems)
-    copies[0].wait()
-    copies[1].wait()
+def lines_kernel(coarse_hbm, lines_ref, coarse_ref, strided, sems):
+    (copy,) = fetch(((coarse_hbm, coarse_ref),), sems)
+    held, coarse = coarse_ref.shape
+    blocks = coarse // LANES
+    strided[...] = jnp.zeros_like(strided)
+    copy.wait()
+    for b in range(blocks):
+        strided[pl.ds(b, held, stride=blocks), :] = coarse_ref[:, b * LANES : (b + 1) * LANES]
+    lines_ref[...] = strided[: lines_ref.shape[0]].astype(BF)
+
+
+def line_count(held, coarse):
+    return -(-held * coarse // LANES // 16) * 16
+
+
+def own_lines(coarse_inverse):
+    count = line_count(*coarse_inverse.shape)
+    return pl.pallas_call(
+        lines_kernel,
+        in_specs=[IN_HBM],
+        out_shape=jax.ShapeDtypeStruct((count, LANES), BF),
+        scratch_shapes=[
+            pltpu.VMEM(coarse_inverse.shape, F32),
+            pltpu.VMEM((2 * count, LANES), F32),
+            pltpu.SemaphoreType.DMA((1,)),
+        ],
+        compiler_params=params(60),
+    )(coarse_inverse)
+
+
+def first_kernel(basis_hbm, orient_hbm, wide_ref, narrow_ref, basis_ref, orient_ref, sems):
+    copies = fetch(((basis_hbm, basis_ref), (orient_hbm, orient_ref)), sems)
+    for copy in copies:
+        copy.wait()
     face = orient_ref.shape[1]
     for row, out in ((0, wide_ref), (1, narrow_ref)):
         order = one_hot(orient_ref[row : row + 1, :], face)
         part = padded(basis_ref[:, (2 + row) * face : (3 + row) * face])
         out[...] = dot_nt(part, order).astype(BF)
-    held, coarse = coarse_ref.shape
-    blocks = coarse // LANES
-    strided[...] = jnp.zeros_like(strided)
-    copies[2].wait()
-    for b in range(blocks):
-        strided[pl.ds(b, held, stride=blocks), :] = coarse_ref[:, b * LANES : (b + 1) * LANES]
-    lines_ref[...] = strided[: lines_ref.shape[0]].astype(BF)
-
-
-def line_count(held, coarse):
-    return -(-held * coarse // LANES // 16) * 16
-
-
-def first(basis, orient, coarse_inverse):
-    face = orient.shape[1]
-    shape = jax.ShapeDtypeStruct((SLOT, face), BF)
-    lines = (line_count(*coarse_inverse.shape), LANES)
-    inputs = (basis, orient, coarse_inverse)
+
+
+def first(basis, orient):
+    shape = jax.ShapeDtypeStruct((SLOT, orient.shape[1]), BF)
+    inputs = (basis, orient)
     return pl.pallas_call(
         first_kernel,
         in_specs=[IN_HBM] * len(inputs),
-        out_shape=[shape, shape, jax.ShapeDtypeStruct(lines, BF)],
-        scratch_shapes=[pltpu.VMEM(a.shape, a.dtype) for a in inputs]
-        + [pltpu.VMEM((2 * lines[0], LANES), F32), pltpu.SemaphoreType.DMA((len(inputs),))],
+        out_shape=[shape, shape],
+        scratch_shapes=[pltpu.VMEM(a.shape, a.dtype) for a in inputs] + [pltpu.SemaphoreType.DMA((len(inputs),))],
         compiler_params=params(60),
     )(*inputs)
 
@@ -134,7 +148,7 @@
         out_specs=[pl.BlockSpec((block, face), by_rows)] * 2,
         out_shape=[half, half],
         compiler_params=params(),
-        cost_estimate=cost(2 * res.size, 4 * res.size),
+        cost_estimate=cost(40000 * res.size, 4 * res.size),
     )(res, share)
 
 
@@ -179,7 +193,7 @@
         ],
         out_specs=pl.BlockSpec((block, LANES), lambda i: (i, 0)),
         out_shape=jax.ShapeDtypeStruct((rows, LANES), BF),
-        compiler_params=params(16),
+        compiler_params=params(60),
         cost_estimate=cost(4 * res.size * LANES, 2 * res.size),
     )(res, share, basis, basis_wide, basis_narrow)
 
@@ -245,6 +259,7 @@
             pltpu.VMEM((NX * LANES, blocks * LANES), BF),
         ],
         compiler_params=params(16),
+        cost_estimate=cost(100_000_000_000, 4_000_000),
     )(parts, *lines)
 
 
@@ -399,30 +414,33 @@
     held, coarse = coarse_inverse.shape
     chunk = rows // WIDE
 
-    mine_wide, mine_narrow, lines = first(basis, ori, coarse_inverse)
+    lines = own_lines(coarse_inverse)
+    other = exchange(lines, 4)
+    mine_wide, mine_narrow = first(after(basis, lines), ori)
     basis_wide = shift(mine_wide, WIDE_AXES, -1)
     basis_narrow = shift(mine_narrow, NARROW_AXES, -1)
-    other = exchange(lines, 4)
-
-    face_wide, face_narrow = outgoing(after(res, mine_wide), share)
-    got_wide = shift(face_wide, WIDE_AXES, 1)
+    lines = jnp.concatenate([lines, after(other, mine_wide)], axis=0)
+    other = exchange(lines, 2)
+
+    primal = primal_parts(after(res, lines), share, basis, basis_wide, basis_narrow)
+    lines = jnp.concatenate([after(lines, primal), other], axis=0)
+    other = exchange(lines, 1)
+    chunks = lax.all_to_all(after(primal, lines).reshape(WIDE, chunk, LANES), WIDE_AXES, 0, 0)
+
+    face_wide, face_narrow = outgoing(after(res, lines), share)
     got_narrow = shift(face_narrow, NARROW_AXES, 1)
-
-    primal = primal_parts(after(res, face_wide), share, basis, basis_wide, basis_narrow)
-    lines = jnp.concatenate([after(lines, primal), other], axis=0)
-    other = exchange(lines, 2)
-    chunks = lax.all_to_all(after(primal, lines).reshape(WIDE, chunk, LANES), WIDE_AXES, 0, 0)
-
-    columns = patch_columns(after(primal_index, primal))
+    columns = patch_columns(after(primal_index, face_wide))
     high, low = columns >> 7, columns & 127
     high_held, low_held = held_place(columns, held)
 
     lines = jnp.concatenate([after(lines, high, high_held), other], axis=0)
-    lines = jnp.concatenate([lines, exchange(lines, 1)], axis=0)
-    pieces = [lines] + [shift(lines, "x", k) for k in range(1, NX)]
+    from_next = shift(lines, "x", -1)
+    from_last = shift(lines, "x", 1)
 
     partial = scatter(after(chunks, lines), high, low, coarse // LANES)
-    parts = lax.all_gather(partial, NARROW_AXES)
+    got_wide = shift(after(face_wide, partial), WIDE_AXES, 1)
+    pieces = [lines, from_last, shift(from_next, "x", -1), from_next]
+    parts = lax.all_gather(after(partial, from_next), NARROW_AXES)
     corr = solve(parts, pieces)
 
     gathered, send_wide, send_narrow = faces(res, share, after(got_wide, corr), got_narrow, ori, inverse)

time: 115 us -> 108 us (0.939); the launches traced: 113 us -> 108 us
  waiting for transfers between devices: 19.1 us -> 14.3 us
  starting transfers between devices: 41 us -> 37.8 us
  Pallas kernels: 31 us -> 32.8 us
    ppermute x12, waiting for transfers between devices: 13.4 us -> 5.76 us  [permute(): return lax.ppermute(array, axes, [(i, target(i)) for i in range(count)])]
    all_to_all x1, starting transfers between devices: 8.42 us -> 3.86 us  [on_device(): corr = lax.all_to_all(corr, WIDE_AXES, 0, 0).reshape(rows, LANES)]
    ppermute x12, starting transfers between devices: 19.9 us -> 22.5 us  [permute(): return lax.ppermute(array, axes, [(i, target(i)) for i in range(count)])]
    all_to_all x1, waiting for transfers between devices: 5.78 us -> 8.08 us  [on_device(): corr = lax.all_to_all(corr, WIDE_AXES, 0, 0).reshape(rows, LANES)]
    all_to_all x1, starting transfers between devices: 5.99 us -> 3.99 us  [on_device(): corr = lax.all_to_all(corr, NARROW_AXES, 0, 0)]
    pallas_call x0 -> x1, Pallas kernels: none -> 1.56 us  [own_lines(): pl.pallas_call(lines_kernel, in_specs=[IN_HBM], out_shape=jax.ShapeDtypeS...]
    pallas_call x1, Pallas kernels: 2.12 us -> 3.61 us  [primal_parts(): pl.pallas_call(primal_kernel, grid=(3,), in_specs=[pl.BlockSpec((block, o...]
    pallas_call x1, Pallas kernels: 1.5 us -> 0.33 us  [outgoing(): pl.pallas_call(outgoing_kernel, grid=(3,), in_specs=[pl.BlockSpec((block,...]
  transfers between devices with their start and end apart: 15 -> 15, of which waited for: 3 -> 5; matrix products, arithmetic and copies ran while one was open for 0% -> 2% of each run, Pallas kernels for 23% -> 27%
where the time goes in v2:
time: 108 us
  starting transfers between devices  37.8 us (35%)
  Pallas kernels  32.8 us (30%)
  blocking collectives  17.5 us (16%)
  waiting for transfers between devices  14.3 us (13%)
  local copies, waits for them, and re-layouts  3.89 us (4%)
    ppermute x12, starting transfers between devices, permute(): return lax.ppermute(array, axes, [(i, target(i)) for i in range(count)])  22.5 us
    all_gather x1, blocking collectives, on_device(): parts = lax.all_gather(after(partial, from_next), NARROW_AXES)  17.5 us
    pallas_call x1, Pallas kernels, faces(): pl.pallas_call(faces_kernel, in_specs=[pl.BlockSpec(memory_space=pltpu.VM...  8.76 us
    pallas_call x1, Pallas kernels, owned(): pl.pallas_call(owned_kernel, in_specs=[pl.BlockSpec(memory_space=pltpu.VM...  8.26 us
    all_to_all x1, waiting for transfers between devices, on_device(): corr = lax.all_to_all(corr, WIDE_AXES, 0, 0).reshape(rows, LANES)  8.08 us
    all_to_all x1, starting transfers between devices, on_device(): lax.all_to_all(after(primal, lines).reshape(WIDE, chunk, LANES), WIDE_AXE...  7.43 us
    ppermute x12, waiting for transfers between devices, permute(): return lax.ppermute(array, axes, [(i, target(i)) for i in range(count)])  5.76 us
    all_to_all x1, starting transfers between devices, on_device(): corr = lax.all_to_all(corr, NARROW_AXES, 0, 0)  3.99 us
  transfers between devices with their start and end apart: 15, of which 5 were waited for; matrix products, arithmetic and copies ran while one was open for 2% of the time, Pallas kernels for 27%

profile of v2, /device:TPU:1, one launch (start us, length us, event | category | flops | bytes accessed | tf_op | source)
XLA Modules:
  0.0 107.5 jit_solution(1174522517758914000)
XLA Ops:
  0.0 1.6 %shard_map.73 = bf16[176,128]{1,0:T(8,128)(2,1)} custom-call(f32[9,2304]{1,0:T(8,128)} %coarse_hbm.1), custom_call_target="tpu_custom_call" | custom-call | tf_op jit(solution)/shard_map/pallas_call | solution.py:95
  1.6 7.8 %collective-permute-start = (bf16[176,128]{1,0:T(8,128)(2,1)}, bf16[176,128]{1,0:T(8,128)(2,1)S(1)}, u32[]{:S(2)}, u32[]{:S(2)}) collective-permute-start(bf16[176,128]{1,0:T(8,128)(2,1)} %shard_map.73), channel_id=1, source_target_pairs={{0,32},{8,40},{16,48},{24,56},{32,0},{40,8},{48,16},{56,24},{1,33}... | collective-permute-start | bytes 135176 | tf_op jit(solution)/shard_map/ppermute | solution.py:26
  9.4 1.9 %shard_map.74 = (bf16[32,512]{1,0:T(8,128)(2,1)}, bf16[32,512]{1,0:T(8,128)(2,1)}) custom-call(bf16[24,2048]{1,0:T(8,128)(2,1)} %bitcast.21, s32[2,512]{1,0:T(2,128)} %bitcast.30), custom_call_target="tpu_custom_call" | custom-call | tf_op jit(solution)/shard_map/pallas_call | solution.py:122
  11.4 1.0 collective-permute-start.2
  12.3 2.0 %collective-permute-start.1 = (bf16[32,512]{1,0:T(8,128)(2,1)}, bf16[32,512]{1,0:T(8,128)(2,1)S(1)}, u32[]{:S(2)}, u32[]{:S(2)}) collective-permute-start(bf16[32,512]{1,0:T(8,128)(2,1)} %get-tuple-element.29), channel_id=1, source_target_pairs={{0,248},{8,0},{16,8},{24,16},{32,24},{40,32},{48,40},{56,48},{64,5... | collective-permute-start | bytes 98312 | tf_op jit(solution)/shard_map/ppermute | solution.py:26
  16.5 3.6 %shard_map.75 = bf16[768,128]{1,0:T(8,128)(2,1)} custom-call(bf16[768,1024]{1,0:T(8,128)(2,1)} %bitcast.17, bf16[1,1024]{1,0:T(2,128)(2,1)} %share_ref.7, bf16[24,2048]{1,0:T(8,128)(2,1)} %bitcast.22, bf16[32,512]{1,0:T(8,128)(2,1)} %copy-done.5, bf16[32,512]{1,0:T(8,128)(2,1)} %copy-done.3), custom_call_target="tpu_custom_call" | custom-call | flops 402653184 | bytes 1572864 | tf_op jit(solution)/shard_map/pallas_call | solution.py:184
  21.0 7.4 %all-to-all-start = ((bf16[32,24,128]{2,1,0:T(8,128)(2,1)}), bf16[32,24,128]{2,1,0:T(8,128)(2,1)S(1)}, u32[]{:S(2)}, u32[]{:S(2)}) async-start(bf16[32,24,128]{2,1,0:T(8,128)(2,1)} %bitcast.28), calls=%async_computation | async-start | bytes 393216 | tf_op jit(solution)/shard_map/all_to_all | solution.py:428
  29.6 0.9 constant_dynamic-update-slice_fusion.2.refs_0_
  30.6 2.6 %collective-permute-start.6 = (bf16[1408,128]{1,0:T(8,128)(2,1)S(1)}, bf16[1408,128]{1,0:T(8,128)(2,1)S(1)}, u32[]{:S(2)}, u32[]{:S(2)}) collective-permute-start(bf16[1408,128]{1,0:T(8,128)(2,1)S(1)} %constant_dynamic-update-slice_fusion.2.refs_0_), channel_id=1, source_target_pairs={{0,192},{64,0},{128,64},{192,128},{1,193},{65,1},{129,65},{193,129... | collective-permute-start | bytes 1081352 | tf_op jit(solution)/shard_map/ppermute | solution.py:26
  33.2 4.2 %collective-permute-start.9 = (bf16[768,512]{1,0:T(8,128)(2,1)S(1)}, bf16[768,512]{1,0:T(8,128)(2,1)}, u32[]{:S(2)}, u32[]{:S(2)}) collective-permute-start(bf16[768,512]{1,0:T(8,128)(2,1)S(1)} %get-tuple-element.43), channel_id=1, source_target_pairs={{0,1},{1,2},{2,3},{3,4},{4,5},{5,6},{6,7},{7,0},{8,9},{9,10},{10,1... | collective-permute-start | bytes 2359304 | tf_op jit(solution)/shard_map/ppermute | solution.py:26
  37.9 1.4 %shard_map.77 = bf16[18,24,128]{2,1,0:T(8,128)(2,1)S(1)} custom-call(bf16[32,24,128]{2,1,0:T(8,128)(2,1)S(1)} %all-to-all-done.refs_0_, s32[32,128]{1,0:T(8,128)S(1)} %get-tuple-element.57.refs_1_, s32[32,128]{1,0:T(8,128)S(1)} %get-tuple-element.55.refs_2_), custom_call_target="tpu_custom_call" | custom-call | tf_op jit(solution)/shard_map/pallas_call | solution.py:219
  39.3 1.5 %collective-permute-start.5 = (bf16[768,512]{1,0:T(8,128)(2,1)S(1)}, bf16[768,512]{1,0:T(8,128)(2,1)}, u32[]{:S(2)}, u32[]{:S(2)}) collective-permute-start(bf16[768,512]{1,0:T(8,128)(2,1)S(1)} %get-tuple-element.40), channel_id=1, source_target_pairs={{0,8},{8,16},{16,24},{24,32},{32,40},{40,48},{48,56},{56,64},{64,7... | collective-permute-start | bytes 2359304 | tf_op jit(solution)/shard_map/ppermute | solution.py:26
  40.8 2.3 %collective-permute-start.8 = (bf16[1408,128]{1,0:T(8,128)(2,1)S(1)}, bf16[1408,128]{1,0:T(8,128)(2,1)S(1)}, u32[]{:S(2)}, u32[]{:S(2)}) collective-permute-start(bf16[1408,128]{1,0:T(8,128)(2,1)S(1)} %collective-permute-done.6.refs_3_), channel_id=1, source_target_pairs={{0,192},{64,0},{128,64},{192,128},{1,193},{65,1},{129,65},{193,129... | collective-permute-start | bytes 1081352 | tf_op jit(solution)/shard_map/ppermute | solution.py:26
  43.1 17.5 %all-gather = bf16[144,24,128]{2,1,0:T(8,128)(2,1)S(1)} all-gather(bf16[18,24,128]{2,1,0:T(8,128)(2,1)S(1)} %shard_map.77), channel_id=2, replica_groups=mesh['x'=4,'z'=8,'y'=4,'core'=2] {'y','core'}, dimensions={0}, use_global_device_ids=true | all-gather | bytes 995328 | tf_op jit(solution)/shard_map/all_gather | solution.py:443
  60.6 5.3 %collective-permute-done.7.refs_1_ = bf16[1408,128]{1,0:T(8,128)(2,1)S(1)} collective-permute-done((bf16[1408,128]{1,0:T(8,128)(2,1)S(1)}, bf16[1408,128]{1,0:T(8,128)(2,1)S(1)}, u32[]{:S(2)}, u32[]{:S(2)}) %collective-permute-start.7) | collective-permute-done | bytes 360480 | tf_op jit(solution)/shard_map/ppermute | solution.py:26
  65.9 1.9 %shard_map.78 = bf16[8,4,24,128]{3,2,1,0:T(8,128)(2,1)} custom-call(bf16[8,18,24,128]{3,2,1,0:T(8,128)(2,1)S(1)} %bitcast.20, bf16[1408,128]{1,0:T(8,128)(2,1)S(1)} %constant_dynamic-update-slice_fusion.2.refs_0_, bf16[1408,128]{1,0:T(8,128)(2,1)S(1)} %collective-permute-done.7.refs_1_, bf16[1408,128]{1,0:T(8,128)(2,1)S(1)} %collective-permute-done.8.refs_2_, ...), custom_call_target="tpu_custom_call" | custom-call | flops 99999997952 | bytes 4000000 | tf_op jit(solution)/shard_map/pallas_call | solution.py:254
  67.8 4.0 %all-to-all-start.1 = ((bf16[8,4,24,128]{3,2,1,0:T(8,128)(2,1)}), bf16[8,4,24,128]{3,2,1,0:T(8,128)(2,1)S(1)}, u32[]{:S(2)}, u32[]{:S(2)}) async-start(bf16[8,4,24,128]{3,2,1,0:T(8,128)(2,1)} %shard_map.78), calls=%async_computation.1 | async-start | bytes 393216 | tf_op jit(solution)/shard_map/all_to_all | solution.py:447
  71.8 8.8 %shard_map.79 = (bf16[768,2048]{1,0:T(8,128)(2,1)}, bf16[768,512]{1,0:T(8,128)(2,1)}, bf16[768,512]{1,0:T(8,128)(2,1)}) custom-call(bf16[768,1024]{1,0:T(8,128)(2,1)} %bitcast.18, bf16[1,1024]{1,0:T(2,128)(2,1)} %share_ref.7, bf16[768,512]{1,0:T(8,128)(2,1)} %collective-permute-done.5.got_wide_ref, bf16[768,512]{1,0:T(8,128)(2,1)} %collective-permute-done.9.got_narrow_ref, ...), custom_call_target="tpu_custom_call" | custom-call | flops 4831838208 | bytes 7340032 | tf_op jit(solution)/shard_map/pallas_call | solution.py:321
  80.8 2.5 %shard_map.80 = bf16[32,24,128]{2,1,0:T(8,128)(2,1)} custom-call(bf16[768,128]{1,0:T(8,128)(2,1)S(1)} %bitcast.25, s32[32,128]{1,0:T(8,128)S(1)} %get-tuple-element.56.refs_1_, s32[32,128]{1,0:T(8,128)S(1)} %get-tuple-element.51.refs_2_), custom_call_target="tpu_custom_call" | custom-call | tf_op jit(solution)/shard_map/pallas_call | solution.py:280
  83.3 3.9 %all-to-all-start.2 = ((bf16[32,24,128]{2,1,0:T(8,128)(2,1)}), bf16[32,24,128]{2,1,0:T(8,128)(2,1)S(1)}, u32[]{:S(2)}, u32[]{:S(2)}) async-start(bf16[32,24,128]{2,1,0:T(8,128)(2,1)} %shard_map.80), calls=%async_computation.2 | async-start | bytes 393216 | tf_op jit(solution)/shard_map/all_to_all | solution.py:452
  87.2 8.3 %shard_map.81.local_ref = bf16[768,1024]{1,0:T(8,128)(2,1)} custom-call(bf16[768,2048]{1,0:T(8,128)(2,1)} %get-tuple-element.47.gathered_ref, bf16[2048,2048]{1,0:T(8,128)(2,1)} %bitcast.27), custom_call_target="tpu_custom_call" | custom-call | flops 3221225472 | bytes 10485760 | tf_op jit(solution)/shard_map/pallas_call | solution.py:344
  95.5 8.1 %all-to-all-done.2 = bf16[32,24,128]{2,1,0:T(8,128)(2,1)S(1)} async-done(((bf16[32,24,128]{2,1,0:T(8,128)(2,1)}), bf16[32,24,128]{2,1,0:T(8,128)(2,1)S(1)}, u32[]{:S(2)}, u32[]{:S(2)}) %all-to-all-start.2) | async-done | bytes 196640 | tf_op jit(solution)/shard_map/all_to_all | solution.py:452
  103.6 1.4 %copy-done = bf16[768,1024]{1,0:T(8,128)(2,1)S(1)} copy-done((bf16[768,1024]{1,0:T(8,128)(2,1)S(1)}, bf16[768,1024]{1,0:T(8,128)(2,1)}, u32[]{:S(2)}) %copy-start) | copy-done | bytes 1572888
  105.0 2.5 %shard_map.82 = bf16[1,768,1024]{2,1,0:T(8,128)(2,1)} custom-call(bf16[768,1024]{1,0:T(8,128)(2,1)S(1)} %copy-done, bf16[768,512]{1,0:T(8,128)(2,1)S(1)} %collective-permute-done.10.back_wide_ref, bf16[768,512]{1,0:T(8,128)(2,1)S(1)} %collective-permute-done.11.back_narrow_ref, bf16[768,128]{1,0:T(8,128)(2,1)S(1)} %bitcast.24, ...), custom_call_target="tpu_custom_call" | custom-call | tf_op jit(solution)/shard_map/pallas_call | solution.py:369
  (51 shorter events, 4.9 us)
Async XLA Ops:
  1.6 26.9 %copy-start.1 = (bf16[1,768,1024]{2,1,0:T(8,128)(2,1)S(1)}, bf16[1,768,1024]{2,1,0:T(8,128)(2,1)}, u32[]{:S(2)}) copy-start(bf16[1,768,1024]{2,1,0:T(8,128)(2,1)} %param.7) | copy-start | bytes 4718596
  1.6 26.9 %copy-start.7 = (bf16[1,1024]{1,0:T(2,128)(2,1)S(1)}, bf16[1,1024]{1,0:T(2,128)(2,1)}, u32[]{:S(2)}) copy-start(bf16[1,1024]{1,0:T(2,128)(2,1)} %share_ref.7) | copy-start | bytes 6148
  1.6 12.8 %collective-permute-start = (bf16[176,128]{1,0:T(8,128)(2,1)}, bf16[176,128]{1,0:T(8,128)(2,1)S(1)}, u32[]{:S(2)}, u32[]{:S(2)}) collective-permute-start(bf16[176,128]{1,0:T(8,128)(2,1)} %shard_map.73), channel_id=1, source_target_pairs={{0,32},{8,40},{16,48},{24,56},{32,0},{40,8},{48,16},{56,24},{1,33}... | collective-permute-start | bytes 135176 | tf_op jit(solution)/shard_map/ppermute | solution.py:26
  11.4 4.0 %collective-permute-start.2 = (bf16[32,512]{1,0:T(8,128)(2,1)}, bf16[32,512]{1,0:T(8,128)(2,1)S(1)}, u32[]{:S(2)}, u32[]{:S(2)}) collective-permute-start(bf16[32,512]{1,0:T(8,128)(2,1)} %get-tuple-element.32), channel_id=1, source_target_pairs={{0,7},{1,0},{2,1},{3,2},{4,3},{5,4},{6,5},{7,6},{8,15},{9,8},{10,9... | collective-permute-start | bytes 98312 | tf_op jit(solution)/shard_map/ppermute | solution.py:26
  12.3 3.4 %collective-permute-start.1 = (bf16[32,512]{1,0:T(8,128)(2,1)}, bf16[32,512]{1,0:T(8,128)(2,1)S(1)}, u32[]{:S(2)}, u32[]{:S(2)}) collective-permute-start(bf16[32,512]{1,0:T(8,128)(2,1)} %get-tuple-element.29), channel_id=1, source_target_pairs={{0,248},{8,0},{16,8},{24,16},{32,24},{40,32},{48,40},{56,48},{64,5... | collective-permute-start | bytes 98312 | tf_op jit(solution)/shard_map/ppermute | solution.py:26
  15.2 4.9 %collective-permute-start.3 = (bf16[352,128]{1,0:T(8,128)(2,1)S(1)}, bf16[352,128]{1,0:T(8,128)(2,1)S(1)}, u32[]{:S(2)}, u32[]{:S(2)}) collective-permute-start(bf16[352,128]{1,0:T(8,128)(2,1)S(1)} %pad_maximum_fusion), channel_id=1, source_target_pairs={{0,16},{8,24},{16,0},{24,8},{32,48},{40,56},{48,32},{56,40},{1,17}... | collective-permute-start | bytes 270344 | tf_op jit(solution)/shard_map/ppermute | solution.py:26
  15.3 0.6 copy-start.3
  20.2 9.5 %collective-permute-start.4 = (bf16[704,128]{1,0:T(8,128)(2,1)S(1)}, bf16[704,128]{1,0:T(8,128)(2,1)}, u32[]{:S(2)}, u32[]{:S(2)}) collective-permute-start(bf16[704,128]{1,0:T(8,128)(2,1)S(1)} %constant_dynamic-update-slice_fusion), channel_id=1, source_target_pairs={{0,8},{8,0},{16,24},{24,16},{32,40},{40,32},{48,56},{56,48},{1,9},... | collective-permute-start | bytes 540680 | tf_op jit(solution)/shard_map/ppermute | solution.py:26
  21.0 16.9 %all-to-all-start = ((bf16[32,24,128]{2,1,0:T(8,128)(2,1)}), bf16[32,24,128]{2,1,0:T(8,128)(2,1)S(1)}, u32[]{:S(2)}, u32[]{:S(2)}) async-start(bf16[32,24,128]{2,1,0:T(8,128)(2,1)} %bitcast.28), calls=%async_computation | async-start | bytes 393216 | tf_op jit(solution)/shard_map/all_to_all | solution.py:428
  28.5 0.7 copy-start.9
  30.6 10.2 %collective-permute-start.6 = (bf16[1408,128]{1,0:T(8,128)(2,1)S(1)}, bf16[1408,128]{1,0:T(8,128)(2,1)S(1)}, u32[]{:S(2)}, u32[]{:S(2)}) collective-permute-start(bf16[1408,128]{1,0:T(8,128)(2,1)S(1)} %constant_dynamic-update-slice_fusion.2.refs_0_), channel_id=1, source_target_pairs={{0,192},{64,0},{128,64},{192,128},{1,193},{65,1},{129,65},{193,129... | collective-permute-start | bytes 1081352 | tf_op jit(solution)/shard_map/ppermute | solution.py:26
  33.2 38.7 %collective-permute-start.9 = (bf16[768,512]{1,0:T(8,128)(2,1)S(1)}, bf16[768,512]{1,0:T(8,128)(2,1)}, u32[]{:S(2)}, u32[]{:S(2)}) collective-permute-start(bf16[768,512]{1,0:T(8,128)(2,1)S(1)} %get-tuple-element.43), channel_id=1, source_target_pairs={{0,1},{1,2},{2,3},{3,4},{4,5},{5,6},{6,7},{7,0},{8,9},{9,10},{10,1... | collective-permute-start | bytes 2359304 | tf_op jit(solution)/shard_map/ppermute | solution.py:26
  37.4 28.5 %collective-permute-start.7 = (bf16[1408,128]{1,0:T(8,128)(2,1)S(1)}, bf16[1408,128]{1,0:T(8,128)(2,1)S(1)}, u32[]{:S(2)}, u32[]{:S(2)}) collective-permute-start(bf16[1408,128]{1,0:T(8,128)(2,1)S(1)} %constant_dynamic-update-slice_fusion.2.refs_0_), channel_id=1, source_target_pairs={{0,64},{64,128},{128,192},{192,0},{1,65},{65,129},{129,193},{193,1... | collective-permute-start | bytes 1081352 | tf_op jit(solution)/shard_map/ppermute | solution.py:26
  39.3 32.6 %collective-permute-start.5 = (bf16[768,512]{1,0:T(8,128)(2,1)S(1)}, bf16[768,512]{1,0:T(8,128)(2,1)}, u32[]{:S(2)}, u32[]{:S(2)}) collective-permute-start(bf16[768,512]{1,0:T(8,128)(2,1)S(1)} %get-tuple-element.40), channel_id=1, source_target_pairs={{0,8},{8,16},{16,24},{24,32},{32,40},{40,48},{48,56},{56,64},{64,7... | collective-permute-start | bytes 2359304 | tf_op jit(solution)/shard_map/ppermute | solution.py:26
  40.8 25.1 %collective-permute-start.8 = (bf16[1408,128]{1,0:T(8,128)(2,1)S(1)}, bf16[1408,128]{1,0:T(8,128)(2,1)S(1)}, u32[]{:S(2)}, u32[]{:S(2)}) collective-permute-start(bf16[1408,128]{1,0:T(8,128)(2,1)S(1)} %collective-permute-done.6.refs_3_), channel_id=1, source_target_pairs={{0,192},{64,0},{128,64},{192,128},{1,193},{65,1},{129,65},{193,129... | collective-permute-start | bytes 1081352 | tf_op jit(solution)/shard_map/ppermute | solution.py:26
  67.8 12.8 %all-to-all-start.1 = ((bf16[8,4,24,128]{3,2,1,0:T(8,128)(2,1)}), bf16[8,4,24,128]{3,2,1,0:T(8,128)(2,1)S(1)}, u32[]{:S(2)}, u32[]{:S(2)}) async-start(bf16[8,4,24,128]{3,2,1,0:T(8,128)(2,1)} %shard_map.78), calls=%async_computation.1 | async-start | bytes 393216 | tf_op jit(solution)/shard_map/all_to_all | solution.py:447
  80.6 23.0 %collective-permute-start.10 = (bf16[768,512]{1,0:T(8,128)(2,1)}, bf16[768,512]{1,0:T(8,128)(2,1)S(1)}, u32[]{:S(2)}, u32[]{:S(2)}) collective-permute-start(bf16[768,512]{1,0:T(8,128)(2,1)} %get-tuple-element.48), channel_id=1, source_target_pairs={{0,248},{8,0},{16,8},{24,16},{32,24},{40,32},{48,40},{56,48},{64,5... | collective-permute-start | bytes 2359304 | tf_op jit(solution)/shard_map/ppermute | solution.py:26
  80.7 22.9 %collective-permute-start.11 = (bf16[768,512]{1,0:T(8,128)(2,1)}, bf16[768,512]{1,0:T(8,128)(2,1)S(1)}, u32[]{:S(2)}, u32[]{:S(2)}) collective-permute-start(bf16[768,512]{1,0:T(8,128)(2,1)} %get-tuple-element.50), channel_id=1, source_target_pairs={{0,7},{1,0},{2,1},{3,2},{4,3},{5,4},{6,5},{7,6},{8,15},{9,8},{10,9... | collective-permute-start | bytes 2359304 | tf_op jit(solution)/shard_map/ppermute | solution.py:26
  83.3 20.3 %all-to-all-start.2 = ((bf16[32,24,128]{2,1,0:T(8,128)(2,1)}), bf16[32,24,128]{2,1,0:T(8,128)(2,1)S(1)}, u32[]{:S(2)}, u32[]{:S(2)}) async-start(bf16[32,24,128]{2,1,0:T(8,128)(2,1)} %shard_map.80), calls=%async_computation.2 | async-start | bytes 393216 | tf_op jit(solution)/shard_map/all_to_all | solution.py:452
  87.2 16.4 %copy-start.2 = (bf16[1,24,2048]{2,1,0:T(8,128)(2,1)S(1)}, bf16[1,24,2048]{2,1,0:T(8,128)(2,1)}, u32[]{:S(2)}) copy-start(bf16[1,24,2048]{2,1,0:T(8,128)(2,1)} %param.11) | copy-start | bytes 294916
  87.2 16.4 %copy-start.4 = (bf16[32,512]{1,0:T(8,128)(2,1)S(1)}, bf16[32,512]{1,0:T(8,128)(2,1)}, u32[]{:S(2)}) copy-start(bf16[32,512]{1,0:T(8,128)(2,1)} %copy-done.3) | copy-start | bytes 98308
  87.2 16.4 %copy-start.6 = (bf16[32,512]{1,0:T(8,128)(2,1)S(1)}, bf16[32,512]{1,0:T(8,128)(2,1)}, u32[]{:S(2)}) copy-start(bf16[32,512]{1,0:T(8,128)(2,1)} %copy-done.5) | copy-start | bytes 98308
  87.2 16.4 %copy-start.8 = (bf16[1,1024]{1,0:T(2,128)(2,1)S(1)}, bf16[1,1024]{1,0:T(2,128)(2,1)}, u32[]{:S(2)}) copy-start(bf16[1,1024]{1,0:T(2,128)(2,1)} %share_ref.7) | copy-start | bytes 6148
  103.6 1.4 %copy-start = (bf16[768,1024]{1,0:T(8,128)(2,1)S(1)}, bf16[768,1024]{1,0:T(8,128)(2,1)}, u32[]{:S(2)}) copy-start(bf16[768,1024]{1,0:T(8,128)(2,1)} %shard_map.81.local_ref) | copy-start | bytes 4718596
  (1 other events, 0.6 us)
